TPU v7x, 128 devices: a whole 4x4x4 slice. The times are simulated.
128 devices in a mesh: dom: 16 (over y_hi, x, core), rep: 8 (over z, y_lo).
Axes of the slice: x: 4, y: 4 (y_hi: 2, y_lo: 2; y = y_hi * 2 + y_lo), z: 4, core: 2. Of those that a mesh axis runs over, the one named last changes fastest.
Arguments:
- features: bfloat16 [24576, 256], P(('dom', 'rep')), may hold values from -6 to 6
- weight: bfloat16 [256, 256], replicated, may hold values from -0.375 to 0.375
- bias: float32 [256], replicated, may hold values from -3 to 3
- adj_tiles: bfloat16 [192, 16, 8, 128, 128], P('dom', None, 'rep'), may hold values from -0.078125 to 0.078125
- adj_cols: int32 [192, 16, 8], P('dom', None, 'rep'), may hold values from 0 to 11, as said below
- degree: int32 [192, 16], P('dom'), may hold values from 1 to 8, as said below
- grad_out: bfloat16 [24576, 256], P(('dom', 'rep')), may hold values from -6 to 6
Outputs:
- activated: bfloat16 [24576, 256], P(('dom', 'rep'))
- feature_grad: bfloat16 [24576, 256], P(('dom', 'rep'))
- weight_grad: float32 [256, 256], replicated
- bias_grad: float32 [256], replicated
Inputs may be any that keep to these rules, and one draw needn't show every extreme that they name: `degree`: in every source shard column some block row uses all 8 slots; most block rows use fewer, and low slots are used more often than high ones. `adj_cols`: within one block row and one source shard the 8 entries are distinct.
All inputs are finite; a program needn't handle non-finite values.
Results may differ from a plain program's by a relative error of at most 0.018.
Values may be sent and summed in bfloat16 or wider, within the bound.
A program may use at most 128 MiB of HBM per device.

v0:
```python
import math

import jax
import jax.numpy as jnp
from jax import lax
from jax.sharding import PartitionSpec as P


def smooth_gate(inputs):
    return jax.nn.gelu(inputs, approximate=True)


def body(features, weight, bias, adj_tiles, adj_cols, degree, grad_out):
    shard_depth = adj_tiles.shape[0]
    cycle_size = lax.axis_size("dom")
    group_size = lax.axis_size("rep")
    slot_count = adj_tiles.shape[2]
    tile_edge = adj_tiles.shape[-1]
    hidden = features.shape[1]
    shard_rows = shard_depth * tile_edge
    replica = lax.axis_index("rep")
    slot_ids = replica * slot_count + jnp.arange(slot_count, dtype=jnp.int32)
    used_mask = (slot_ids[None, None, :] < degree[:, :, None]).astype(adj_tiles.dtype)
    tile_vals = adj_tiles * used_mask[:, :, :, None, None]
    shard_features = lax.all_gather(features, "rep", axis=0, tiled=True)
    arrived = lax.all_gather(shard_features, "dom", axis=0, tiled=True)
    shard_count = arrived.shape[0] // shard_rows
    arrived_blocks = arrived.reshape(shard_count, shard_depth, tile_edge, hidden)

    def gather_add_shard(shard_step, inner):
        source = lax.dynamic_index_in_dim(arrived_blocks, shard_step, 0, False)
        part_tiles = lax.dynamic_index_in_dim(tile_vals, shard_step, 1, False)
        part_cols = lax.dynamic_index_in_dim(adj_cols, shard_step, 1, False)
        selected = jnp.take(source, part_cols, axis=0)
        return inner + jnp.einsum(
            "bkxy,bkyf->bxf", part_tiles, selected, preferred_element_type=jnp.float32
        )

    partial_value = lax.fori_loop(
        0, shard_count, gather_add_shard, jnp.zeros((shard_depth, tile_edge, hidden), jnp.float32)
    )
    summed = lax.psum_scatter(
        partial_value.reshape(shard_rows, hidden), "rep", scatter_dimension=0, tiled=True
    )
    aggregated = summed.astype(jnp.bfloat16)
    preact = jnp.dot(aggregated, weight, preferred_element_type=jnp.float32) + bias
    activated, pullback = jax.vjp(smooth_gate, preact)
    delta = pullback(grad_out.astype(jnp.float32))[0].astype(jnp.bfloat16)
    grad_scale = 1.0 / math.sqrt(aggregated.shape[0] * cycle_size * group_size)
    weight_term = lax.dot_general(
        aggregated, delta, (((0,), (0,)), ((), ())), preferred_element_type=jnp.float32
    )
    bias_term = jnp.sum(delta.astype(jnp.float32), axis=0)
    weight_sum, bias_sum = lax.psum((weight_term, bias_term), ("dom", "rep"))
    spread = lax.dot_general(
        delta, weight, (((1,), (1,)), ((), ())), preferred_element_type=jnp.float32
    ).astype(jnp.bfloat16)
    shard_spread = lax.all_gather(spread, "rep", axis=0, tiled=True)
    swapped_tiles, swapped_cols = (
        lax.all_to_all(tile_vals, "dom", split_axis=1, concat_axis=1, tiled=True),
        lax.all_to_all(
            adj_cols.astype(jnp.bfloat16), "dom", split_axis=1, concat_axis=1, tiled=True
        ),
    )
    target_cols = swapped_cols.astype(jnp.int32)
    arrived = lax.all_gather(shard_spread, "dom", axis=0, tiled=True)
    shard_count = arrived.shape[0] // shard_rows
    back_arrived_blocks = arrived.reshape(shard_count, shard_depth, tile_edge, hidden)

    def back_add_shard(shard_step, inner):
        source = lax.dynamic_index_in_dim(back_arrived_blocks, shard_step, 0, False)
        part_tiles = lax.dynamic_index_in_dim(swapped_tiles, shard_step, 1, False)
        part_cols = lax.dynamic_index_in_dim(target_cols, shard_step, 1, False)
        product = jnp.einsum(
            "bkxy,bxf->bkyf", part_tiles, source, preferred_element_type=jnp.float32
        )
        return inner.at[part_cols].add(product)

    backward = lax.fori_loop(
        0, shard_count, back_add_shard, jnp.zeros((shard_depth, tile_edge, hidden), jnp.float32)
    )
    grads = lax.psum_scatter(
        backward.reshape(shard_rows, hidden).astype(jnp.bfloat16),
        "rep",
        scatter_dimension=0,
        tiled=True,
    )
    return (activated.astype(jnp.bfloat16), grads, weight_sum * grad_scale, bias_sum * grad_scale)


def solution(mesh):
    return jax.shard_map(
        body,
        mesh=mesh,
        in_specs=(
            P(("dom", "rep"), None),
            P(),
            P(),
            P("dom", None, "rep", None, None),
            P("dom", None, "rep"),
            P("dom", None),
            P(("dom", "rep"), None),
        ),
        out_specs=(P(("dom", "rep"), None), P(("dom", "rep"), None), P(), P()),
        check_vma=False,
    )
```

profile of v0, /device:TPU:0, one launch (start us, length us, event | category | flops | bytes accessed | tf_op | source)
XLA Modules:
  0.0 611.2 jit_solution(4591500914087671087)
XLA Ops:
  7.2 34.7 %all_gather.12 = bf16[1536,256]{1,0:T(8,128)(2,1)} all-gather(bf16[192,256]{1,0:T(8,128)(2,1)} %param.11), channel_id=1, replica_groups=mesh['dom'=16,'rep'=8] {'rep'}, dimensions={0}, use_global_device_ids=true | all-gather | bytes 884736 | tf_op jit(solution)/shard_map/all_gather | solution.py:25
  42.2 5.9 copy_multiply_fusion
  48.1 85.9 %all-gather.3.cloned.1.call-done = bf16[24576,256]{1,0:T(8,128)(2,1)} async-done(((bf16[1536,256]{1,0:T(8,128)(2,1)}), bf16[24576,256]{1,0:T(8,128)(2,1)}) %all-gather.3.cloned.1.call-update) | async-done | bytes 12582928 | tf_op jit(solution)/shard_map/all_gather | solution.py:26
  134.0 59.8 %while.28 = (s32[]{:T(128)}, f32[12,128,256]{2,1,0:T(8,128)S(1)}, bf16[12,16,1,128,128]{4,3,0,2,1:T(8,128)(2,1)}, s32[12,16,1]{0,2,1:T(1,128)S(1)}, bf16[16,12,1...) while((s32[]{:T(128)}, f32[12,128,256]{2,1,0:T(8,128)S(1)}, ...), condition=%wide.region_1.2_spmd.clone, body=%wide.region_0.1_spmd.clone.sunk | while | flops 101844040 | bytes 7475523 | solution.py:39
  135.8 1.9 select_add_fusion.2
  139.5 1.9 select_add_fusion.2
  143.3 1.9 select_add_fusion.2
  147.0 1.9 select_add_fusion.2
  150.7 1.9 select_add_fusion.2
  154.5 1.9 select_add_fusion.2
  158.2 1.9 select_add_fusion.2
  162.0 1.9 select_add_fusion.2
  165.7 1.9 select_add_fusion.2
  195.0 42.5 %reduce-scatter.3.cloned.1.call-done = f32[192,256]{1,0:T(8,128)} async-done(((f32[1536,256]{1,0:T(8,128)}), f32[192,256]{1,0:T(8,128)}) %reduce-scatter.3.cloned.1.call-update) | async-done | bytes 196624 | tf_op jit(solution)/shard_map/reduce_scatter | solution.py:42
  237.5 1.9 convert_reduce_fusion
  239.6 33.2 %all_gather.14 = bf16[1536,256]{1,0:T(8,128)(2,1)} all-gather(bf16[192,256]{1,0:T(8,128)(2,1)S(1)} %convolution_convert_fusion), channel_id=1, replica_groups=mesh['dom'=16,'rep'=8] {'rep'}, dimensions={0}, use_global_device_ids=true | all-gather | bytes 884736 | tf_op jit(solution)/shard_map/all_gather | solution.py:58
  272.9 13.8 %all_to_all.10 = bf16[12,16,1]{0,2,1:T(2,128)(2,1)S(1)} all-to-all(bf16[12,16,1]{0,2,1:T(2,128)(2,1)S(1)} %copy.14), channel_id=1, replica_groups=mesh['dom'=16,'rep'=8] {'dom'}, dimensions={1} | all-to-all | bytes 768 | tf_op jit(solution)/shard_map/all_to_all | solution.py:61
  286.7 4.8 all-to-all-start.1
  292.6 95.5 %all-to-all-done.1 = bf16[12,16,1,128,128]{4,3,0,2,1:T(8,128)(2,1)} async-done(((bf16[12,16,1,128,128]{4,3,0,2,1:T(8,128)(2,1)}), bf16[12,16,1,128,128]{4,3,0,2,1:T(8,128)(2,1)}, u32[]{:S(2)}, u32[]{:S(2)}) %all-to-all-start.1) | async-done | bytes 6291488 | tf_op jit(solution)/shard_map/all_to_all | solution.py:60
  388.1 30.0 %all-gather.5.cloned.1.call-done = bf16[24576,256]{1,0:T(8,128)(2,1)} async-done(((bf16[1536,256]{1,0:T(8,128)(2,1)}), bf16[24576,256]{1,0:T(8,128)(2,1)}) %all-gather.5.cloned.1.call-update) | async-done | bytes 12582928 | tf_op jit(solution)/shard_map/all_gather | solution.py:66
  418.3 57.1 %while.27 = (s32[]{:T(128)}, f32[12,128,256]{2,1,0:T(8,128)S(1)}, s32[12,16,1]{0,2,1:T(1,128)S(1)}, bf16[12,16,1,128,128]{4,3,0,2,1:T(8,128)(2,1)}, bf16[16,12,128,256]{3,2,1,0:T(8,128)(2,1)}, /*index=5*/s32[]{:T(128)}) while((s32[]{:T(128)}, f32[12,128,256]{2,1,0:T(8,128)S(1)}, s32[12,16,1]{0,2,1:T(1,128)S(1)}, ...), condition=%wide.region_5.6_spmd, body=%wide.region_3.5_spmd.sunk | while | flops 101056552 | bytes 7472353 | solution.py:79
  476.4 65.6 %psum.15 = f32[256]{0:T(256)S(1)} all-reduce(f32[256]{0:T(256)S(1)} %get-tuple-element.244), channel_id=1, replica_groups=mesh['dom'=16,'rep'=8] {'dom','rep'}, use_global_device_ids=true, to_apply=%region_9.10 | all-reduce | flops 256 | bytes 2048 | tf_op jit(solution)/shard_map/psum | solution.py:54
  542.6 22.3 %all-reduce.2.cloned.1.call-done = f32[256,256]{1,0:T(8,128)} async-done(((f32[256,256]{1,0:T(8,128)}), f32[256,256]{1,0:T(8,128)}) %all-reduce.2.cloned.1.call-update) | async-done | bytes 262160 | tf_op jit(solution)/shard_map/psum | solution.py:54
  566.6 38.1 %reduce-scatter.5.cloned.1.call-done = bf16[192,256]{1,0:T(8,128)(2,1)} async-done(((bf16[1536,256]{1,0:T(8,128)(2,1)}), bf16[192,256]{1,0:T(8,128)(2,1)}) %reduce-scatter.5.cloned.1.call-update) | async-done | bytes 98320 | tf_op jit(solution)/shard_map/reduce_scatter | solution.py:82
  (156 shorter events, 104.8 us)
Async XLA Ops:
  7.2 230.3 %copy-start = (bf16[256,256]{1,0:T(8,128)(2,1)S(1)}, bf16[256,256]{1,0:T(8,128)(2,1)}, u32[]{:S(2)}) copy-start(bf16[256,256]{1,0:T(8,128)(2,1)} %param.12) | copy-start | bytes 393220
  7.2 34.8 %copy-start.4 = (s32[12,16]{1,0:T(8,128)S(1)}, s32[12,16]{1,0:T(8,128)}, u32[]{:S(2)}) copy-start(s32[12,16]{1,0:T(8,128)} %param.16) | copy-start | bytes 2308
  7.2 34.9 %copy-start.3 = (s32[12,16,1]{1,2,0:T(1,128)S(1)}, s32[12,16,1]{1,2,0:T(1,128)}, u32[]{:S(2)}) copy-start(s32[12,16,1]{1,2,0:T(1,128)} %param.15) | copy-start | bytes 2308
  7.2 126.8 %all-gather.3.cloned.1.call-start = ((), (), s32[]{:S(2)}) async-start(), calls=%async_computation.4 | async-start | bytes 13369344 | tf_op jit(solution)/shard_map/all_gather | solution.py:26
  41.9 195.6 %reduce-scatter.3.cloned.1.call-start = ((), (), s32[]{:S(2)}) async-start(), calls=%async_computation.5 | async-start | bytes 1769472 | tf_op jit(solution)/shard_map/reduce_scatter | solution.py:42
  193.8 1.2 copy-start.1
  193.8 43.7 %copy-start.5 = (bf16[192,256]{1,0:T(8,128)(2,1)S(1)}, bf16[192,256]{1,0:T(8,128)(2,1)}, u32[]{:S(2)}) copy-start(bf16[192,256]{1,0:T(8,128)(2,1)} %param.17) | copy-start | bytes 294916
  193.8 43.7 %copy-start.6 = (f32[256]{0:T(256)S(1)}, f32[256]{0:T(256)}, u32[]{:S(2)}) copy-start(f32[256]{0:T(256)} %param.13) | copy-start | bytes 3076
  194.9 223.2 %all-gather.5.cloned.1.call-start = ((), (), s32[]{:S(2)}) async-start(), calls=%async_computation.6 | async-start | bytes 13369344 | tf_op jit(solution)/shard_map/all_gather | solution.py:66
  286.7 4.8 copy-start.2
  286.7 101.4 %all-to-all-start.1 = ((bf16[12,16,1,128,128]{4,3,0,2,1:T(8,128)(2,1)}), bf16[12,16,1,128,128]{4,3,0,2,1:T(8,128)(2,1)}, u32[]{:S(2)}, u32[]{:S(2)}) async-start(bf16[12,16,1,128,128]{4,3,0,2,1:T(8,128)(2,1)} %get-tuple-element.359), calls=%async_computation.2 | async-start | bytes 12582912 | tf_op jit(solution)/shard_map/all_to_all | solution.py:60
  291.5 273.4 %all-reduce.2.cloned.1.call-start = ((), (), s32[]{:S(2)}) async-start(), calls=%async_computation.8 | async-start | bytes 524288 | tf_op jit(solution)/shard_map/psum | solution.py:54
  292.6 312.1 %reduce-scatter.5.cloned.1.call-start = ((), (), s32[]{:S(2)}) async-start(), calls=%async_computation.7 | async-start | bytes 884736 | tf_op jit(solution)/shard_map/reduce_scatter | solution.py:82
Sparse Core Ops, SparseCore 0:
  42.1 91.8 all-gather.2
  195.1 42.3 reduce-scatter.2
  272.9 145.1 all-gather.4
  423.3 141.5 all-reduce.1
  567.7 36.8 reduce-scatter.4
where the time goes:
time: 613 us; the launch traced here: 611 us
  waiting for transfers between devices  314 us (51%)
  blocking collectives  147 us (24%)
  matrix products  60 us (10%)
  other arithmetic  39.1 us (6%)
  local copies, waits for them, and re-layouts  30.1 us (5%)
  between operations  13.9 us (2%)
    all_to_all x1, waiting for transfers between devices, body(): lax.all_to_all(tile_vals, 'dom', split_axis=1, concat_axis=1, tiled=True)  95.5 us
    all_gather x1, waiting for transfers between devices, body(): arrived = lax.all_gather(shard_features, 'dom', axis=0, tiled=True)  85.9 us
    psum x1, blocking collectives, body(): weight_sum, bias_sum = lax.psum((weight_term, bias_term), ('dom', 'rep'))  65.6 us
    reduce_scatter x1, waiting for transfers between devices, body(): lax.psum_scatter(partial_value.reshape(shard_rows, hidden), 'rep', scatte...  42.5 us
    reduce_scatter x1, waiting for transfers between devices, body(): lax.psum_scatter(backward.reshape(shard_rows, hidden).astype(jnp.bfloat16...  38.1 us
    all_gather x1, blocking collectives, body(): shard_features = lax.all_gather(features, 'rep', axis=0, tiled=True)  34.7 us
    all_gather x1, blocking collectives, body(): shard_spread = lax.all_gather(spread, 'rep', axis=0, tiled=True)  33.2 us
    dot_general x16, matrix products, gather_add_shard(): jnp.einsum('bkxy,bkyf->bxf', part_tiles, selected, preferred_element_type...  30.1 us
  transfers between devices with their start and end apart: 6, of which 6 were waited for; matrix products, arithmetic and copies ran while one was open for 11% of the time, Pallas kernels for 0%

commit v1 on v0

v1 whole, which is shorter than its diff:
```python
import math

import jax
import jax.numpy as jnp
from jax import lax
from jax.experimental import pallas as pl
from jax.experimental.pallas import tpu as pltpu
from jax.sharding import PartitionSpec as P

MESH = pl.DeviceIdType.MESH
BF16, F32, I32 = jnp.bfloat16, jnp.float32, jnp.int32
RING, SIDE = 4, 64
BLOCKS, SHARDS, EDGE, HID = 12, 8, 128, 256
CHUNK = 192
REPS, DOMS = 8, 16
NONE = BLOCKS
ROOT = math.sqrt(2.0 / math.pi)
CUBIC = 0.044715


def wrap(value, size):
    return lax.rem(value, size)


def place(part, x, y, z):
    at = (x, y, z)
    return part * 64 + at[(part + 2) % 3] * 16 + at[(part + 1) % 3] * 4 + at[part]


def kernel(scale, feat, weight, bias, tiles, meta, grad_out,
           act_out, fgrad_out, wgrad_out, bgrad_out,
           own, swapped, flipped, table_in, table, gathered,
           theirs, arrived, mine, shares, landed, spread,
           chain, grads, lands_c, lands_b, lands_a,
           wterm, wland, wdom, wall,
           ag_send, ag_recv, rs_send, rs_recv, core_send, core_recv, local_sem,
           rep_send, rep_recv, spr_send, spr_recv, fwd_send, fwd_recv,
           w1_send, w1_recv, w2_send, w2_recv, w3_send, w3_recv):
    dom, rep = lax.axis_index("dom"), lax.axis_index("rep")
    core = wrap(dom, 2)
    x = wrap(lax.div(dom, 2), 4)
    y_hi = lax.div(dom, 8)
    z, y_lo = lax.div(rep, 2), wrap(rep, 2)
    y = y_hi * 2 + y_lo
    at = (x, y, z)

    def device(px, py, pz, pc):
        return ((lax.div(py, 2) * 4 + px) * 2 + pc, pz * 2 + wrap(py, 2))

    def near(axis, step):
        to = list(at)
        to[axis] = wrap(at[axis] + step, RING)
        return device(*to, core)

    partner = (dom + 1 - 2 * core, rep)

    barrier = pltpu.get_barrier_semaphore()
    for k in range(1, REPS):
        pl.semaphore_signal(barrier, inc=1, device_id=(dom, wrap(rep + k, REPS)), device_id_type=MESH)
    for k in range(1, DOMS):
        pl.semaphore_signal(barrier, inc=1, device_id=(wrap(dom + k, DOMS), rep), device_id_type=MESH)
    for step in (1, 3):
        pl.semaphore_signal(barrier, inc=1, device_id=near(1, step), device_id_type=MESH)
    pl.semaphore_wait(barrier, REPS - 1 + DOMS - 1 + 2)

    started = []

    def send(src, dst, send_sem, recv_sem, target):
        copy = pltpu.make_async_remote_copy(
            src_ref=src, dst_ref=dst, send_sem=send_sem, recv_sem=recv_sem, device_id=target, device_id_type=MESH)
        copy.start()
        started.append(copy)
        return copy

    def half(ref, phase, part, e, h):
        axis = (at[part], at[(part + 1) % 3], at[(part + 2) % 3])
        if phase == 0:
            return ref.at[part * 64 + axis[2] * 16 + axis[1] * 4 + e, pl.ds(32 * h, 32)]
        if phase == 1:
            return ref.at[pl.ds(part * 64 + axis[2] * 16 + e * 4 + 2 * h, 2)]
        return ref.at[pl.ds(part * 64 + e * 16 + 8 * h, 8)]

    def ag_sem(phase, part, way, k):
        return ((phase * 3 + part) * 2 + way) * 3 + k

    def ag_copy(phase, part, way, k, go):
        axis = (part + phase) % 3
        m = at[axis]
        target = near(axis, 1 if way == 0 else 3)
        sem = ag_sem(phase, part, way, k)
        if go:
            e = m if k < 2 else wrap(m + (3 if way == 0 else 1), RING)
        else:
            back = (3 if way == 0 else 1) * (1 if k < 2 else 2)
            e = wrap(m + back, RING)
        h = way if k in (0, 2) else 1 - way
        ref = half(gathered, phase, part, e, h)
        if go:
            send(ref, ref, ag_send.at[sem], ag_recv.at[sem], target)
        else:
            pltpu.make_async_remote_copy(
                src_ref=ref, dst_ref=ref, send_sem=ag_send.at[sem], recv_sem=ag_recv.at[sem],
                device_id=target, device_id_type=MESH).wait_recv()

    def ag_each(phase, k, go):
        for part in range(3):
            for way in range(2):
                ag_copy(phase, part, way, k, go)

    def flip(which, first, count):
        def body(b, carry):
            for s in range(SHARDS):
                flipped[which, b, pl.ds(s * EDGE, EDGE), :] = jnp.transpose(swapped[which, b * SHARDS + s])
            return carry
        lax.fori_loop(first, first + count, body, 0)

    for part in range(3):
        gathered[place(part, x, y, z)] = feat[pl.ds(part * SIDE, SIDE), :]
    gathered[192] = jnp.zeros((SIDE, HID), BF16)
    ag_each(0, 0, True)
    ag_each(0, 1, True)
    table_copy = send(meta.at[1 - core], table_in, core_send.at[0], core_recv.at[0], partner)
    tile_copy = send(tiles.at[:, 1 - core], swapped.at[1], core_send.at[1], core_recv.at[1], partner)
    own_table = pltpu.make_async_copy(meta.at[core], table.at[0], local_sem.at[0])
    own_table.start()
    own_tiles = pltpu.make_async_copy(tiles.at[:, core], swapped.at[0], local_sem.at[1])
    own_tiles.start()
    ag_each(0, 0, False)
    ag_each(0, 2, True)
    own_tiles.wait()
    flip(0, 0, 1)
    ag_each(0, 1, False)
    ag_each(0, 2, False)
    ag_each(1, 0, True)
    ag_each(1, 1, True)
    flip(0, 1, 2)
    ag_each(1, 0, False)
    ag_each(1, 2, True)
    flip(0, 3, 2)
    ag_each(1, 1, False)
    ag_each(1, 2, False)
    ag_each(2, 0, True)
    ag_each(2, 1, True)
    flip(0, 5, 6)
    ag_each(2, 0, False)
    ag_each(2, 2, True)
    own_table.wait()
    table_copy.wait_recv()
    their_table = pltpu.make_async_copy(table_in, table.at[1], local_sem.at[2])
    their_table.start()
    flip(0, 11, 1)
    tile_copy.wait_recv()
    flip(1, 0, 12)
    their_table.wait()
    ag_each(2, 1, False)
    ag_each(2, 2, False)

    def row_block(which, b):
        lhs = jnp.concatenate([swapped[which, b * SHARDS + s] for s in range(SHARDS)], axis=1)
        rhs = jnp.concatenate([gathered[table[which, b, k]] for k in range(2 * SHARDS)], axis=0)
        return jnp.dot(lhs, rhs, preferred_element_type=F32)

    def their_block(b, carry):
        theirs[pl.ds(pl.multiple_of(b * EDGE, EDGE), EDGE), :] = row_block(1, b).astype(BF16)
        return carry

    def my_block(b, carry):
        mine[pl.ds(pl.multiple_of(b * EDGE, EDGE), EDGE), :] = row_block(0, b)
        return carry

    swap = []
    for part in range(4):
        lax.fori_loop(part * 3, part * 3 + 3, their_block, 0)
        rows = pl.ds(part * 384, 384)
        swap.append(send(theirs.at[rows], arrived.at[rows], core_send.at[2 + part], core_recv.at[2 + part], partner))
    lax.fori_loop(0, BLOCKS, my_block, 0)
    for copy in swap:
        copy.wait_recv()

    def rows_of(peer):
        return pl.ds(pl.multiple_of(peer * CHUNK, CHUNK), CHUNK)

    slots = []
    for k in range(1, REPS):
        to = wrap(rep + k, REPS)
        rows = rows_of(to)
        shares[to] = (mine[rows, :] + arrived[rows, :].astype(F32)).astype(BF16)
        slots.append(send(shares.at[to], landed.at[rep], rep_send.at[k], rep_recv.at[k], (dom, to)))
    total = mine[rows_of(rep), :] + arrived[rows_of(rep), :].astype(F32)
    for k in range(1, REPS):
        slots[k - 1].wait_recv()
        total = total + landed[wrap(rep + REPS - k, REPS)].astype(F32)

    aggregated = total.astype(BF16)
    v = jnp.dot(aggregated, weight[...], preferred_element_type=F32) + bias[...]
    t = jnp.tanh(ROOT * (v + CUBIC * (v * v * v)))
    act_out[...] = (0.5 * v * (1.0 + t)).astype(BF16)
    slope = 0.5 * (1.0 + t) + 0.5 * v * ((1.0 - t) * (1.0 + t)) * (ROOT * (1.0 + 3.0 * CUBIC * (v * v)))
    delta = (grad_out[...].astype(F32) * slope).astype(BF16)
    spread[0, rows_of(rep), :] = lax.dot_general(
        delta, weight[...], (((1,), (1,)), ((), ())), preferred_element_type=F32).astype(BF16)
    here = spread.at[0, rows_of(rep)]
    spread_in = []
    for k in range(1, REPS):
        spread_in.append(send(here, here, spr_send.at[k], spr_recv.at[k], (dom, wrap(rep + k, REPS))))
    forward_in = [send(here, spread.at[1, rows_of(rep)], fwd_send.at[0], fwd_recv.at[0], partner)]

    wsum = lax.dot_general(aggregated, delta, (((0,), (0,)), ((), ())), preferred_element_type=F32)
    bsum = jnp.sum(delta.astype(F32).reshape(CHUNK // 8, 8, HID), axis=0)
    for r in range(REPS):
        wterm[r, 0:32, :] = wsum[r * 32:(r + 1) * 32, :]
        wterm[r, 32:40, :] = bsum
    wland[rep] = wterm[rep]

    for k in range(1, REPS):
        spread_in[k - 1].wait_recv()
        rows = rows_of(wrap(rep + REPS - k, REPS))
        forward_in.append(send(spread.at[0, rows], spread.at[1, rows], fwd_send.at[k], fwd_recv.at[k], partner))
    w1 = []
    for k in range(1, REPS):
        to = wrap(rep + k, REPS)
        w1.append(send(wterm.at[to], wland.at[rep], w1_send.at[k], w1_recv.at[k], (dom, to)))

    for s in range(2):
        for which in range(2):
            chain[s, which * 13 + NONE] = jnp.zeros((EDGE, HID), F32)

    def link(g, which):
        def body(b, carry):
            rows = pl.ds(pl.multiple_of(g * 2 * EDGE, 2 * EDGE), 2 * EDGE)
            product = jnp.dot(
                flipped[which, b, rows, :], spread[which, pl.ds(pl.multiple_of(b * EDGE, EDGE), EDGE), :],
                preferred_element_type=F32)
            for s in range(2):
                before = table[which, b, 2 * SHARDS + g * 2 + s]
                chain[s, which * 13 + b] = product[s * EDGE:(s + 1) * EDGE] + chain[s, which * 13 + before]
            return carry
        lax.fori_loop(0, BLOCKS, body, 0)

    def close(g):
        for s in range(2):
            shard = g * 2 + s
            sy, sx = lax.div(shard, 4), wrap(shard, 4)
            for c in range(BLOCKS):
                both = (chain[s, table[0, c, 3 * SHARDS + shard]]
                        + chain[s, 13 + table[1, c, 3 * SHARDS + shard]]).astype(BF16)
                for h in range(2):
                    q = 2 * c + h
                    r = q // 3
                    grads[place(q % 3, sx, sy * 2 + r % 2, r // 2)] = both[h * SIDE:(h + 1) * SIDE]

    link(0, 0)
    for copy in forward_in:
        copy.wait_recv()
    link(0, 1)
    close(0)

    def shard_pair(g, carry):
        link(g, 0)
        link(g, 1)
        close(g)
        return carry

    lax.fori_loop(1, 4, shard_pair, 0)

    for copy in w1:
        copy.wait_recv()
    wdom[dom] = sum(wland[r] for r in range(REPS))
    w2 = []
    for k in range(1, DOMS):
        w2.append(send(wdom.at[dom], wdom.at[dom], w2_send.at[k], w2_recv.at[k], (wrap(dom + k, DOMS), rep)))

    lands = (lands_a, lands_b, lands_c)

    def rs_copy(phase, part, way, k, go):
        axis = (part + phase) % 3
        m = at[axis]
        sem = ag_sem(phase, part, way, k)
        e = wrap(m + (2 if k == 0 else (1 if way == 0 else 3)), RING)
        h = way if k in (0, 2) else 1 - way
        land = lands[phase].at[(part * 2 + way) * 3 + k]
        target = near(axis, 1 if way == 0 else 3)
        if go:
            send(half(grads, phase, part, e, h), land, rs_send.at[sem], rs_recv.at[sem], target)
        else:
            pltpu.make_async_remote_copy(
                src_ref=land, dst_ref=land, send_sem=rs_send.at[sem], recv_sem=rs_recv.at[sem],
                device_id=target, device_id_type=MESH).wait_recv()

    def rs_each(phase, k, go):
        for part in range(3):
            for way in range(2):
                rs_copy(phase, part, way, k, go)

    def reduce(phase):
        rs_each(phase, 0, True)
        rs_each(phase, 1, True)
        for part in range(3):
            for way in range(2):
                axis = (part + phase) % 3
                rs_copy(phase, part, way, 0, False)
                to = half(grads, phase, part, wrap(at[axis] + (1 if way == 0 else 3), RING), way)
                to[...] = (to[...].astype(F32)
                           + lands[phase][(part * 2 + way) * 3].astype(F32)).astype(BF16)
                rs_copy(phase, part, way, 2, True)

    def settle(phase):
        for part in range(3):
            axis = (part + phase) % 3
            for way in range(2):
                rs_copy(phase, part, way, 1, False)
            for way in range(2):
                rs_copy(phase, part, way, 2, False)
            for h in range(2):
                ref = half(grads, phase, part, at[axis], h)
                full = (ref[...].astype(F32) + lands[phase][(part * 2 + h) * 3 + 2].astype(F32)
                        + lands[phase][(part * 2 + 1 - h) * 3 + 1].astype(F32)).astype(BF16)
                if phase == 0:
                    fgrad_out[pl.ds(part * SIDE + 32 * h, 32), :] = full
                else:
                    ref[...] = full

    reduce(2)
    settle(2)

    for copy in w2:
        copy.wait_recv()
    wfull = sum(wdom[d] for d in range(DOMS)) * scale
    wall[rep] = wfull[0:32]
    bgrad_out[...] = jnp.sum(wfull[32:40], axis=0, keepdims=True)
    w3 = []
    for k in range(1, REPS):
        w3.append(send(wall.at[rep], wall.at[rep], w3_send.at[k], w3_recv.at[k], (dom, wrap(rep + k, REPS))))

    reduce(1)
    settle(1)
    reduce(0)
    settle(0)
    for copy in w3:
        copy.wait_recv()
    for r in range(REPS):
        wgrad_out[pl.ds(r * 32, 32), :] = wall[r]
    for copy in started:
        copy.wait_send()


def tables(adj_cols, degree):
    rep = lax.axis_index("rep")
    cols = adj_cols[:, :, 0]
    used = rep < degree
    shard = jnp.arange(SHARDS, dtype=I32)[None, :, None, None]
    half = jnp.arange(2, dtype=I32)[None, None, None, :]
    q = 2 * cols.reshape(BLOCKS, SHARDS, 2, 1) + half
    part, r = q % 3, q // 3
    x, y, z = shard % 4 + 0 * r, (shard // 4) * 2 + r % 2, r // 2
    where = jnp.where(
        part == 0, place(0, x, y, z), jnp.where(part == 1, place(1, x, y, z), place(2, x, y, z)))
    where = jnp.where(used.reshape(BLOCKS, SHARDS, 2, 1), where, 192)
    where = where.transpose(2, 0, 1, 3).reshape(2, BLOCKS, 2 * SHARDS)
    blocks = jnp.arange(BLOCKS, dtype=I32)
    same = (cols[:, None, :] == cols[None, :, :]) & used[None, :, :] & (blocks[None, :, None] < blocks[:, None, None])
    before = jnp.max(jnp.where(same, blocks[None, :, None], -1), axis=1)
    hit = (cols[None, :, :] == blocks[:, None, None]) & used[None, :, :]
    last = jnp.max(jnp.where(hit, blocks[None, :, None], -1), axis=1)
    ends = [jnp.where(a < 0, NONE, a).reshape(BLOCKS, SHARDS, 2).transpose(2, 0, 1) for a in (before, last)]
    meta = jnp.concatenate([where] + ends, axis=2).astype(I32)
    return jnp.pad(meta, ((0, 0), (0, 4), (0, 96)))


def body(features, weight, bias, adj_tiles, adj_cols, degree, grad_out):
    vmem = pl.BlockSpec(memory_space=pltpu.VMEM)
    dma = pltpu.SemaphoreType.DMA
    rows = BLOCKS * EDGE
    scale = 1.0 / math.sqrt(CHUNK * REPS * DOMS)
    call = pl.pallas_call(
        lambda *refs: kernel(scale, *refs),
        out_shape=(
            jax.ShapeDtypeStruct((CHUNK, HID), BF16),
            jax.ShapeDtypeStruct((CHUNK, HID), BF16),
            jax.ShapeDtypeStruct((HID, HID), F32),
            jax.ShapeDtypeStruct((1, HID), F32),
        ),
        in_specs=[vmem, vmem, vmem, pl.BlockSpec(memory_space=pl.ANY), vmem, vmem],
        out_specs=(vmem, vmem, vmem, vmem),
        scratch_shapes=[
            pltpu.VMEM((8, 128), F32),
            pltpu.VMEM((2, BLOCKS * SHARDS, EDGE, EDGE), BF16),
            pltpu.VMEM((2, BLOCKS, SHARDS * EDGE, EDGE), BF16),
            pltpu.VMEM((16, 128), I32),
            pltpu.SMEM((2, 16, 128), I32),
            pltpu.VMEM((193, SIDE, HID), BF16),
            pltpu.VMEM((rows, HID), BF16),
            pltpu.VMEM((rows, HID), BF16),
            pltpu.VMEM((rows, HID), F32),
            pltpu.VMEM((REPS, CHUNK, HID), BF16),
            pltpu.VMEM((REPS, CHUNK, HID), BF16),
            pltpu.VMEM((2, rows, HID), BF16),
            pltpu.VMEM((2, 26, EDGE, HID), F32),
            pltpu.VMEM((192, SIDE, HID), BF16),
            pltpu.VMEM((18, 8, SIDE, HID), BF16),
            pltpu.VMEM((18, 2, SIDE, HID), BF16),
            pltpu.VMEM((18, 32, HID), BF16),
            pltpu.VMEM((REPS, 40, HID), F32),
            pltpu.VMEM((REPS, 40, HID), F32),
            pltpu.VMEM((DOMS, 40, HID), F32),
            pltpu.VMEM((REPS, 32, HID), F32),
            dma((54,)), dma((54,)), dma((54,)), dma((54,)), dma((6,)), dma((6,)), dma((3,)),
            dma((REPS,)), dma((REPS,)), dma((REPS,)), dma((REPS,)), dma((REPS,)), dma((REPS,)),
            dma((REPS,)), dma((REPS,)), dma((DOMS,)), dma((DOMS,)), dma((REPS,)), dma((REPS,)),
        ],
        compiler_params=pltpu.CompilerParams(
            collective_id=0, has_side_effects=True, vmem_limit_bytes=56 * 1024 * 1024),
    )
    act, fgrad, wgrad, bgrad = call(
        features, weight, bias.reshape(1, HID),
        adj_tiles.reshape(BLOCKS * SHARDS, 2, EDGE, EDGE), tables(adj_cols, degree), grad_out)
    return act, fgrad, wgrad, bgrad.reshape(HID)


def solution(mesh):
    return jax.shard_map(
        body,
        mesh=mesh,
        in_specs=(
            P(("dom", "rep"), None),
            P(),
            P(),
            P("dom", None, "rep", None, None),
            P("dom", None, "rep"),
            P("dom", None),
            P(("dom", "rep"), None),
        ),
        out_specs=(P(("dom", "rep"), None), P(("dom", "rep"), None), P(), P()),
        check_vma=False,
    )
```

time: 613 us -> 145 us (0.24)
  waiting for transfers between devices: 314 us -> 0 us
  blocking collectives: 147 us -> 0 us
  Pallas kernels: 0 us -> 134 us
  matrix products: 60 us -> 0 us
  other arithmetic: 39.1 us -> 0.99 us
  local copies, waits for them, and re-layouts: 30.1 us -> 9.48 us
  between operations: 13.9 us -> 0.71 us
    pallas_call x0 -> x1, Pallas kernels: none -> 134 us  [body(): call(features, weight, bias.reshape(1, HID), adj_tiles.reshape(BLOCKS * S...]
    all_gather x2 -> x0, waiting for transfers between devices: 116 us -> none  [the longest x1 85.9 us: body(): arrived = lax.all_gather(shard_features, 'dom', axis=0, tiled=True)]
    all_to_all x1 -> x0, waiting for transfers between devices: 95.5 us -> none  [body(): lax.all_to_all(tile_vals, 'dom', split_axis=1, concat_axis=1, tiled=True)]
    reduce_scatter x2 -> x0, waiting for transfers between devices: 80.6 us -> none  [the longest x1 42.5 us: body(): lax.psum_scatter(partial_value.reshape(shard_rows, hidden), 'rep', scatte...]
    all_gather x2 -> x0, blocking collectives: 67.9 us -> none  [the longest x1 34.7 us: body(): shard_features = lax.all_gather(features, 'rep', axis=0, tiled=True)]
    psum x1 -> x0, blocking collectives: 65.6 us -> none  [body(): weight_sum, bias_sum = lax.psum((weight_term, bias_term), ('dom', 'rep'))]
    dot_general x35 -> x0, matrix products: 60 us -> none  [the longest x16 30.1 us: gather_add_shard(): jnp.einsum('bkxy,bkyf->bxf', part_tiles, selected, preferred_element_type...]
    scatter-add x16 -> x0, other arithmetic: 29.5 us -> none  [back_add_shard(): return inner.at[part_cols].add(product)]
  transfers between devices with their start and end apart: 6 -> 0, of which waited for: 6 -> 0; matrix products, arithmetic and copies ran while one was open for 11% -> 0% of each run, Pallas kernels for 0% -> 0%
where the time goes in v1:
time: 145 us
  Pallas kernels  134 us (92%)
  local copies, waits for them, and re-layouts  9.48 us (7%)
    pallas_call x1, Pallas kernels, body(): call(features, weight, bias.reshape(1, HID), adj_tiles.reshape(BLOCKS * S...  134 us
    unnamed x6, local copies, waits for them, and re-layouts  7.45 us

profile of v1, /device:TPU:0, one launch (start us, length us, event | category | flops | bytes accessed | tf_op | source)
XLA Modules:
  0.0 144.8 jit_solution(768655851654584251)
XLA Ops:
  0.7 0.7 broadcast_compare_fusion
  1.4 0.1 copy.23
  1.5 0.1 add.161
  1.6 0.1 add.162
  1.7 0.1 add.155
  1.9 0.1 add.168
  2.0 0.1 add.175
  2.1 0.1 add.150
  2.3 0.1 copy.28
  2.4 0.7 copy.37
  3.1 0.1 select_reduce_fusion.1
  3.2 0.1 copy.29
  3.3 0.1 copy.30
  3.4 0.1 copy.32
  3.4 0.1 copy.33
  3.5 0.8 copy.25
  4.3 0.1 copy.27
  4.5 0.1 pad_add_fusion
  4.6 0.6 pad.4.refs_4_
  5.2 133.6 %shard_map.102 = (bf16[192,256]{1,0:T(8,128)(2,1)}, bf16[192,256]{1,0:T(8,128)(2,1)}, f32[256,256]{1,0:T(8,128)}, f32[1,256]{1,0:T(1,128)}) custom-call(bf16[192,256]{1,0:T(8,128)(2,1)} %refs_0_.1, bf16[256,256]{1,0:T(8,128)(2,1)} %refs_1_.1, f32[1,256]{1,0:T(1,128)} %bitcast.29, bf16[96,2,128,128]{3,2,1,0:T(8,128)(2,1)} %bitcast.21, ...), custom_call_target="tpu_custom_call" | custom-call | tf_op jit(solution)/shard_map/pallas_call | solution.py:414
  138.8 1.5 %copy.42 = bf16[192,256]{1,0:T(8,128)(2,1)} copy(bf16[192,256]{1,0:T(8,128)(2,1)} %get-tuple-element.20) | data formatting | bytes 196608
  140.3 1.5 %copy.43 = bf16[192,256]{1,0:T(8,128)(2,1)} copy(bf16[192,256]{1,0:T(8,128)(2,1)} %get-tuple-element.21) | data formatting | bytes 196608
  141.9 1.7 %copy.44 = f32[256,256]{1,0:T(8,128)} copy(f32[256,256]{1,0:T(8,128)} %get-tuple-element.22) | data formatting | bytes 524288
  143.5 1.2 copy.45
  (18 shorter events, 0.4 us)

commit v2 on v0

v2 whole, which is shorter than its diff:
```python
import math

import jax
import jax.numpy as jnp
from jax import lax
from jax.experimental import pallas as pl
from jax.experimental.pallas import tpu as pltpu
from jax.sharding import PartitionSpec as P

MESH = pl.DeviceIdType.MESH
BF16, F32, I32 = jnp.bfloat16, jnp.float32, jnp.int32
RING, SIDE = 4, 64
BLOCKS, SHARDS, EDGE, HID = 12, 8, 128, 256
CHUNK = 192
REPS = 8
NONE = BLOCKS
EMPTY = 192
ROOT = math.sqrt(2.0 / math.pi)
CUBIC = 0.044715


def wrap(value, size):
    return lax.rem(value, size)


def turned(part, x, y, z):
    at = (x, y, z)
    return at[(part + 2) % 3], at[(part + 1) % 3], at[part]


def place(part, x, y, z):
    c, b, a = turned(part, x, y, z)
    return part * 64 + c * 16 + b * 4 + a


def kernel(scale, feat, weight_in, bias_in, tiles, cols_in, degree_in, grad_in,
           act_out, fgrad_out, wgrad_out, bgrad_out,
           weight, bias, cols, degree, grad, act, fgrad,
           swapped, flipped, table_own, table_in, table, gathered,
           theirs, arrived, mine, shares, landed, spread,
           chain, grads, land_z, land_y, land_x, land_1, land_0,
           wterm, wx, wcore_out, wcore, whi_out, whi, wrep, wall, bsum_out,
           sems):
    dom, rep = lax.axis_index("dom"), lax.axis_index("rep")
    core = wrap(dom, 2)
    x = wrap(lax.div(dom, 2), 4)
    y_hi = lax.div(dom, 8)
    z, y_lo = lax.div(rep, 2), wrap(rep, 2)
    y = y_hi * 2 + y_lo
    at = (x, y, z)

    def near(axis, step):
        to = list(at)
        to[axis] = wrap(at[axis] + step, RING)
        return (lax.div(to[1], 2) * 4 + to[0]) * 2 + core, to[2] * 2 + wrap(to[1], 2)

    def peer(k):
        return dom, wrap(rep + k, REPS)

    partner = (dom + 1 - 2 * core, rep)
    across = (wrap(dom + 8, 16), rep)

    barrier = pltpu.get_barrier_semaphore()

    def greet(target):
        pl.semaphore_signal(barrier, inc=1, device_id=target, device_id_type=MESH)

    for axis in range(3):
        for step in (1, 3, 2):
            greet(near(axis, step))
    greet(partner)
    for k in range(1, REPS):
        greet(peer(k))

    used = [0]
    started = []

    def lane(count=1):
        used[0] += count
        return used[0] - count

    def local(src, dst):
        copy = pltpu.make_async_copy(src, dst, sems.at[lane()])
        copy.start()
        return copy

    def remote(src, dst, target, slot=None):
        slot = lane(2) if slot is None else slot
        return pltpu.make_async_remote_copy(
            src_ref=src, dst_ref=dst, send_sem=sems.at[slot], recv_sem=sems.at[slot + 1],
            device_id=target, device_id_type=MESH)

    def send(src, dst, target, slot=None):
        copy = remote(src, dst, target, slot)
        copy.start()
        started.append(copy)
        return copy

    small = [local(cols_in, cols), local(degree_in, degree)]
    pieces = [local(feat.at[pl.ds(part * SIDE, SIDE)], gathered.at[place(part, x, y, z)]) for part in range(3)]
    own_tiles = local(tiles.at[:, core], swapped.at[0])
    dense_in = [local(weight_in, weight), local(bias_in, bias), local(grad_in, grad)]
    gathered[EMPTY] = jnp.zeros((SIDE, HID), BF16)

    pl.semaphore_wait(barrier, 9 + 1 + REPS - 1)

    def row_of(part, c, b):
        return gathered.at[pl.ds(part * 64 + c * 16 + b * 4, 4)]

    def half_of(part, b, h):
        return gathered.at[pl.ds(part * 64 + at[(part + 2) % 3] * 16 + b * 4 + 2 * h, 2)]

    first = []
    for part in range(3):
        for step in (1, 3, 2):
            first.append(send(feat.at[pl.ds(part * SIDE, SIDE)], gathered.at[place(part, x, y, z)], near(part, step)))
    tile_copy = send(tiles.at[:, 1 - core], swapped.at[1], partner)

    for copy in small:
        copy.wait()
    col = cols[:, 0, :]
    live = rep < degree[...]
    shard = lax.div(lax.broadcasted_iota(I32, (BLOCKS, 16), 1), 2)
    shard_x, shard_y = wrap(shard, 4), lax.div(shard, 4) * 2
    block = lax.broadcasted_iota(I32, (BLOCKS, 16), 0)
    table_own[...] = jnp.zeros(table_own.shape, I32)
    for h in range(2):
        q = 2 * col + h
        r = (q * 11) >> 5
        part, to_z = q - 3 * r, r >> 1
        to_y = shard_y + (r - 2 * to_z)
        spot = jnp.where(part == 0, place(0, shard_x, to_y, to_z),
                         jnp.where(part == 1, place(1, shard_x, to_y, to_z), place(2, shard_x, to_y, to_z)))
        table_own[16 * h:16 * h + BLOCKS, 0:16] = jnp.where(live, spot, EMPTY)
    before = jnp.full((BLOCKS, 16), NONE, I32)
    last = jnp.full((BLOCKS, 16), NONE, I32)
    for b in range(BLOCKS):
        here = live[b:b + 1]
        before = jnp.where((col == col[b:b + 1]) & here & (block > b), b, before)
        last = jnp.where((block == col[b:b + 1]) & here, b, last)
    table_own[32:32 + BLOCKS, 0:16] = before
    table_own[48:48 + BLOCKS, 0:16] = last
    table_copy = send(table_own, table_in, partner)
    own_table = local(table_own, table.at[0])

    def flip(which, b0, count):
        def body(b, carry):
            for s in range(SHARDS):
                spot = (s % 4) * 2 + s // 4
                flipped[which, b, pl.ds(spot * EDGE, EDGE), :] = jnp.transpose(swapped[which, b * SHARDS + s])
            return carry
        lax.fori_loop(b0, b0 + count, body, 0)

    for copy in pieces:
        copy.wait()
    for copy in first:
        copy.wait_recv()

    slots_1 = [[[lane(2) for k in range(3)] for way in range(2)] for part in range(3)]
    slots_2 = [[[lane(2) for k in range(6)] for way in range(2)] for part in range(3)]
    FIRST, SECOND = (0, 1), (3, 2)

    def ways():
        for part in range(3):
            for way in range(2):
                yield part, way, (1 if way == 0 else 3)

    def round_1(part, way, step, k, go):
        m = at[(part + 1) % 3]
        h = way if k in (0, 2) else 1 - way
        if go:
            b = m if k < 2 else wrap(m + 4 - step, RING)
        else:
            b = wrap(m + (4 - step) * (1 if k < 2 else 2), RING)
        ref = half_of(part, b, h)
        target, slot = near((part + 1) % 3, step), slots_1[part][way][k]
        if go:
            send(ref, ref, target, slot)
        else:
            remote(ref, ref, target, slot).wait_recv()

    def round_2(part, way, step, k, go):
        m, b0 = at[(part + 2) % 3], at[(part + 1) % 3]
        offset = k if k < 4 else (FIRST if way == 0 else SECOND)[k - 4]
        if go:
            c = m if k < 4 else wrap(m + 4 - step, RING)
        else:
            c = wrap(m + (4 - step) * (1 if k < 4 else 2), RING)
        ref = row_of(part, c, wrap(b0 + offset, RING))
        target, slot = near((part + 2) % 3, step), slots_2[part][way][k]
        if go:
            send(ref, ref, target, slot)
        else:
            remote(ref, ref, target, slot).wait_recv()

    def each(action, k, go):
        for part, way, step in ways():
            action(part, way, step, k, go)

    each(round_1, 0, True)
    each(round_1, 1, True)
    each(round_2, 0, True)
    own_tiles.wait()
    flip(0, 0, 1)
    each(round_1, 0, False)
    each(round_1, 2, True)
    each(round_1, 1, False)
    each(round_2, 1, True)
    each(round_2, 3, True)
    flip(0, 1, 1)
    each(round_2, 0, False)
    for part, way, step in ways():
        if way == 0:
            round_2(part, way, step, 4, True)
    each(round_1, 2, False)
    each(round_2, 2, True)
    flip(0, 2, 4)
    each(round_2, 1, False)
    each(round_2, 3, False)
    for part, way, step in ways():
        if way == 0:
            round_2(part, way, step, 5, True)
        else:
            round_2(part, way, step, 4, True)
    flip(0, 6, 6)
    own_table.wait()
    table_copy.wait_recv()
    their_table = local(table_in, table.at[1])
    tile_copy.wait_recv()
    each(round_2, 2, False)
    for part, way, step in ways():
        if way == 1:
            round_2(part, way, step, 5, True)
    flip(1, 0, 12)
    their_table.wait()
    each(round_2, 4, False)
    each(round_2, 5, False)

    def entry(which, kind, b, s):
        return table[which, kind * 16 + b, 2 * s + core]

    def row_block(which, b):
        lhs = jnp.concatenate([swapped[which, b * SHARDS + s] for s in range(SHARDS)], axis=1)
        rhs = jnp.concatenate([gathered[entry(which, h, b, s)] for s in range(SHARDS) for h in range(2)], axis=0)
        return jnp.dot(lhs, rhs, preferred_element_type=F32)

    def their_block(b, carry):
        theirs[pl.ds(pl.multiple_of(b * EDGE, EDGE), EDGE), :] = row_block(1, b).astype(BF16)
        return carry

    def my_block(b, carry):
        mine[pl.ds(pl.multiple_of(b * EDGE, EDGE), EDGE), :] = row_block(0, b)
        return carry

    swap = []
    for part in range(4):
        lax.fori_loop(part * 3, part * 3 + 3, their_block, 0)
        rows = pl.ds(part * 384, 384)
        swap.append(send(theirs.at[rows], arrived.at[rows], partner))
    lax.fori_loop(0, BLOCKS, my_block, 0)
    for copy in swap:
        copy.wait_recv()

    def rows_of(r):
        return pl.ds(pl.multiple_of(r * CHUNK, CHUNK), CHUNK)

    slots = []
    for k in range(1, REPS):
        to = wrap(rep + k, REPS)
        rows = rows_of(to)
        shares[to] = (mine[rows, :] + arrived[rows, :].astype(F32)).astype(BF16)
        slots.append(send(shares.at[to], landed.at[rep], peer(k)))
    total = mine[rows_of(rep), :] + arrived[rows_of(rep), :].astype(F32)
    for copy in dense_in:
        copy.wait()
    for k in range(1, REPS):
        slots[k - 1].wait_recv()
        total = total + landed[wrap(rep + REPS - k, REPS)].astype(F32)

    aggregated = total.astype(BF16)
    v = jnp.dot(aggregated, weight[...], preferred_element_type=F32) + bias[...]
    t = jnp.tanh(ROOT * (v + CUBIC * (v * v * v)))
    slope = 0.5 * (1.0 + t) + 0.5 * v * ((1.0 - t) * (1.0 + t)) * (ROOT * (1.0 + 3.0 * CUBIC * (v * v)))
    delta = (grad[...].astype(F32) * slope).astype(BF16)
    spread[0, rows_of(rep), :] = lax.dot_general(
        delta, weight[...], (((1,), (1,)), ((), ())), preferred_element_type=F32).astype(BF16)
    here = spread.at[0, rows_of(rep)]
    spread_in = [send(here, here, peer(k)) for k in range(1, REPS)]
    forward_in = [send(here, spread.at[1, rows_of(rep)], partner)]
    act[...] = (0.5 * v * (1.0 + t)).astype(BF16)
    outgoing = [local(act, act_out)]

    wsum = lax.dot_general(aggregated, delta, (((0,), (0,)), ((), ())), preferred_element_type=F32)
    bsum = jnp.sum(delta.astype(F32).reshape(CHUNK // 8, 8, HID), axis=0)
    for k in range(RING):
        wterm[k, 0:64, :] = wsum[k * 64:(k + 1) * 64, :]
        wterm[k, 64:72, :] = bsum
    wx[x] = wterm[x]
    w_x = [send(wterm.at[wrap(x + k, RING)], wx.at[x], near(0, k)) for k in range(1, RING)]

    for k in range(1, REPS):
        spread_in[k - 1].wait_recv()
        rows = rows_of(wrap(rep + REPS - k, REPS))
        forward_in.append(send(spread.at[0, rows], spread.at[1, rows], partner))

    for s in range(2):
        for which in range(2):
            chain[s, which * 13 + NONE] = jnp.zeros((EDGE, HID), F32)

    def link(to_x, which):
        rows = pl.ds(pl.multiple_of(to_x * 2 * EDGE, 2 * EDGE), 2 * EDGE)

        def body(b, carry):
            product = jnp.dot(
                flipped[which, b, rows, :], spread[which, pl.ds(pl.multiple_of(b * EDGE, EDGE), EDGE), :],
                preferred_element_type=F32)
            for s in range(2):
                prior = chain[s, which * 13 + entry(which, 2, b, s * 4 + to_x)]
                chain[s, which * 13 + b] = product[s * EDGE:(s + 1) * EDGE] + prior
            return carry
        lax.fori_loop(0, BLOCKS, body, 0)

    def close(to_x):
        for s in range(2):
            for c in range(BLOCKS):
                both = (chain[s, entry(0, 3, c, s * 4 + to_x)]
                        + chain[s, 13 + entry(1, 3, c, s * 4 + to_x)]).astype(BF16)
                for h in range(2):
                    q = 2 * c + h
                    part, r = q % 3, q // 3
                    grads[(part,) + turned(part, to_x, s * 2 + r % 2, r // 2)] = both[h * SIDE:(h + 1) * SIDE]

    def add_to(ref, *others):
        full = ref[...].astype(F32)
        for other in others:
            full = full + other[...].astype(F32)
        ref[...] = full.astype(BF16)

    slots_q = [[[[lane(2) for k in range(3)] for way in range(2)] for g in range(4)] for part in (0, 2)]
    lands_q = {0: land_z, 2: land_y}

    def quarter(part, plane, to_x, h):
        if part == 0:
            return grads.at[0, plane, pl.ds(2 * h, 2), to_x]
        return grads.at[2, plane, to_x, pl.ds(2 * h, 2)]

    def quarter_copy(part, way, g, k, to_x):
        axis = 2 if part == 0 else 1
        step = 1 if way == 0 else 3
        plane = wrap(at[axis] + (2 if k == 0 else step), RING)
        h = way if k in (0, 2) else 1 - way
        return remote(quarter(part, plane, to_x, h), lands_q[part].at[(g * 2 + way) * 3 + k],
                      near(axis, step), slots_q[part // 2][g][way][k])

    def begin(copy):
        copy.start()
        started.append(copy)

    def quarter_send(g, to_x):
        for k in range(2):
            for part in (0, 2):
                for way in range(2):
                    begin(quarter_copy(part, way, g, k, to_x))

    def quarter_pass(g, to_x):
        for part in (0, 2):
            axis = 2 if part == 0 else 1
            for way in range(2):
                quarter_copy(part, way, g, 0, to_x).wait_recv()
                plane = wrap(at[axis] + (1 if way == 0 else 3), RING)
                add_to(quarter(part, plane, to_x, way), lands_q[part].at[(g * 2 + way) * 3])
                begin(quarter_copy(part, way, g, 2, to_x))

    def quarter_settle(g, to_x):
        for part in (0, 2):
            axis = 2 if part == 0 else 1
            for way in range(2):
                for k in (1, 2):
                    quarter_copy(part, way, g, k, to_x).wait_recv()
            for h in range(2):
                add_to(quarter(part, at[axis], to_x, h), lands_q[part].at[(g * 2 + h) * 3 + 2],
                       lands_q[part].at[(g * 2 + 1 - h) * 3 + 1])

    slots_x = [[lane(2) for k in range(3)] for way in range(2)]

    def plane_copy(way, k):
        step = 1 if way == 0 else 3
        h = way if k in (0, 2) else 1 - way
        return remote(grads.at[1, wrap(x + (2 if k == 0 else step), RING), pl.ds(2 * h, 2)], land_x.at[way * 3 + k],
                      near(0, step), slots_x[way][k])

    def plane_pass(way):
        begin(plane_copy(way, 1))
        plane_copy(way, 0).wait_recv()
        add_to(grads.at[1, wrap(x + (1 if way == 0 else 3), RING), pl.ds(2 * way, 2)], land_x.at[way * 3])
        begin(plane_copy(way, 2))

    def rows_out(part):
        axis = (part + 1) % 3
        out = []
        for k in range(1, RING):
            out.append(send(grads.at[part, at[(part + 2) % 3], wrap(at[axis] + k, RING)], land_1.at[part * 3 + k - 1],
                            near(axis, k)))
        return out

    def rows_in(part, copies):
        for copy in copies:
            copy.wait_recv()
        add_to(grads.at[part, at[(part + 2) % 3], at[(part + 1) % 3]], *[land_1.at[part * 3 + k] for k in range(3)])

    def piece_at(part, a):
        return grads.at[part, at[(part + 2) % 3], at[(part + 1) % 3], a]

    def pieces_out(part):
        return [send(piece_at(part, wrap(at[part] + k, RING)), land_0.at[part * 3 + k - 1], near(part, k))
                for k in range(1, RING)]

    def pieces_in(part, copies):
        for copy in copies:
            copy.wait_recv()
        full = piece_at(part, at[part])[...].astype(F32)
        for k in range(3):
            full = full + land_0[part * 3 + k].astype(F32)
        fgrad[pl.ds(part * SIDE, SIDE), :] = full.astype(BF16)

    turn = [wrap(x + 2, RING), wrap(x + 1, RING), wrap(x + 3, RING), x]

    link(turn[0], 0)
    for copy in forward_in:
        copy.wait_recv()
    link(turn[0], 1)
    close(turn[0])
    quarter_send(0, turn[0])
    begin(plane_copy(0, 0))
    begin(plane_copy(1, 0))
    for copy in w_x:
        copy.wait_recv()
    wsum = wx[0] + wx[1] + wx[2] + wx[3]
    wx[0] = wsum
    wcore_out[0:32, :] = wx[0, pl.ds(pl.multiple_of((1 - core) * 32, 32), 32), :]
    wcore_out[32:40, :] = wx[0, 64:72, :]
    w_core = send(wcore_out, wcore, partner)

    link(turn[1], 0)
    link(turn[1], 1)
    close(turn[1])
    quarter_pass(0, turn[0])
    quarter_send(1, turn[1])
    plane_pass(0)
    w_core.wait_recv()
    wcore[0:32, :] = wcore[0:32, :] + wx[0, pl.ds(pl.multiple_of(core * 32, 32), 32), :]
    wcore[32:40, :] = wcore[32:40, :] + wx[0, 64:72, :]
    whi_out[0:16, :] = wcore[pl.ds(pl.multiple_of((1 - y_hi) * 16, 16), 16), :]
    whi_out[16:24, :] = wcore[32:40, :]
    w_hi = send(whi_out, whi, across)

    link(turn[2], 0)
    link(turn[2], 1)
    close(turn[2])
    quarter_pass(1, turn[1])
    quarter_send(2, turn[2])
    plane_pass(1)
    quarter_settle(0, turn[0])
    w_hi.wait_recv()
    wrep[rep, 0:16, :] = whi[0:16, :] + wcore[pl.ds(pl.multiple_of(y_hi * 16, 16), 16), :]
    wrep[rep, 16:24, :] = whi[16:24, :] + wcore[32:40, :]
    w_rep = [send(wrep.at[rep], wrep.at[rep], peer(k)) for k in range(1, REPS)]

    link(turn[3], 0)
    link(turn[3], 1)
    close(turn[3])
    quarter_send(3, turn[3])
    quarter_pass(2, turn[2])
    quarter_settle(1, turn[1])
    for copy in w_rep:
        copy.wait_recv()
    wfull = wrep[0]
    for r in range(1, REPS):
        wfull = wfull + wrep[r]
    wfull = wfull * scale
    bsum_out[...] = jnp.sum(wfull[16:24], axis=0, keepdims=True)
    outgoing.append(local(bsum_out, bgrad_out))

    def wrows(start, count):
        return wall.at[pl.ds(pl.multiple_of(start, 16), count)]

    wall[pl.ds(pl.multiple_of(x * 64 + core * 32 + y_hi * 16, 16), 16), :] = wfull[0:16]
    ref = wrows(x * 64 + core * 32 + y_hi * 16, 16)
    w_hi = send(ref, ref, across)
    quarter_pass(3, turn[3])
    quarter_settle(2, turn[2])
    w_hi.wait_recv()
    ref = wrows(x * 64 + core * 32, 32)
    w_core = send(ref, ref, partner)

    for way in range(2):
        for k in (1, 2):
            plane_copy(way, k).wait_recv()
    for h in range(2):
        add_to(grads.at[1, x, pl.ds(2 * h, 2)], land_x.at[h * 3 + 2], land_x.at[(1 - h) * 3 + 1])
    rows = {1: rows_out(1)}
    quarter_settle(3, turn[3])
    for part in (0, 2):
        rows[part] = rows_out(part)
    w_core.wait_recv()
    ref = wrows(x * 64, 64)
    w_x = [send(ref, ref, near(0, k)) for k in range(1, RING)]
    last_out = {}
    for part in (1, 0, 2):
        rows_in(part, rows[part])
        last_out[part] = pieces_out(part)
    for copy in w_x:
        copy.wait_recv()
    outgoing.append(local(wall, wgrad_out))
    for part in (1, 0, 2):
        pieces_in(part, last_out[part])
    outgoing.append(local(fgrad, fgrad_out))
    for copy in started:
        copy.wait_send()
    for copy in outgoing:
        copy.wait()


def hand_over(*refs):
    ins, outs, held, sems = refs[:4], refs[4:8], refs[8:12], refs[12]
    copies = [pltpu.make_async_copy(ins[k], held[k], sems.at[k]) for k in range(4)]
    for copy in copies:
        copy.start()
    onward = []
    for k in range(4):
        copies[k].wait()
        onward.append(pltpu.make_async_copy(held[k], outs[k], sems.at[4 + k]))
        onward[k].start()
    for copy in onward:
        copy.wait()


def body(features, weight, bias, adj_tiles, adj_cols, degree, grad_out):
    anywhere = pl.BlockSpec(memory_space=pl.ANY)
    rows = BLOCKS * EDGE
    scale = 1.0 / math.sqrt(CHUNK * REPS * 16)
    outs = (
        jax.ShapeDtypeStruct((CHUNK, HID), BF16),
        jax.ShapeDtypeStruct((CHUNK, HID), BF16),
        jax.ShapeDtypeStruct((HID, HID), F32),
        jax.ShapeDtypeStruct((1, HID), F32),
    )
    call = pl.pallas_call(
        lambda *refs: kernel(scale, *refs),
        out_shape=outs,
        in_specs=[anywhere] * 7,
        out_specs=(anywhere,) * 4,
        scratch_shapes=[
            pltpu.VMEM((HID, HID), BF16),
            pltpu.VMEM((1, HID), F32),
            pltpu.VMEM((BLOCKS, 1, 16), I32),
            pltpu.VMEM((BLOCKS, 16), I32),
            pltpu.VMEM((CHUNK, HID), BF16),
            pltpu.VMEM((CHUNK, HID), BF16),
            pltpu.VMEM((CHUNK, HID), BF16),
            pltpu.VMEM((2, BLOCKS * SHARDS, EDGE, EDGE), BF16),
            pltpu.VMEM((2, BLOCKS, SHARDS * EDGE, EDGE), BF16),
            pltpu.VMEM((64, 128), I32),
            pltpu.VMEM((64, 128), I32),
            pltpu.SMEM((2, 64, 128), I32),
            pltpu.VMEM((193, SIDE, HID), BF16),
            pltpu.VMEM((rows, HID), BF16),
            pltpu.VMEM((rows, HID), BF16),
            pltpu.VMEM((rows, HID), F32),
            pltpu.VMEM((REPS, CHUNK, HID), BF16),
            pltpu.VMEM((REPS, CHUNK, HID), BF16),
            pltpu.VMEM((2, rows, HID), BF16),
            pltpu.VMEM((2, 26, EDGE, HID), F32),
            pltpu.VMEM((3, 4, 4, 4, SIDE, HID), BF16),
            pltpu.VMEM((24, 2, SIDE, HID), BF16),
            pltpu.VMEM((24, 2, SIDE, HID), BF16),
            pltpu.VMEM((6, 2, 4, SIDE, HID), BF16),
            pltpu.VMEM((9, 4, SIDE, HID), BF16),
            pltpu.VMEM((9, SIDE, HID), BF16),
            pltpu.VMEM((RING, 72, HID), F32),
            pltpu.VMEM((RING, 72, HID), F32),
            pltpu.VMEM((40, HID), F32),
            pltpu.VMEM((40, HID), F32),
            pltpu.VMEM((24, HID), F32),
            pltpu.VMEM((24, HID), F32),
            pltpu.VMEM((REPS, 24, HID), F32),
            pltpu.VMEM((HID, HID), F32),
            pltpu.VMEM((1, HID), F32),
            pltpu.SemaphoreType.DMA((512,)),
        ],
        compiler_params=pltpu.CompilerParams(
            collective_id=0, has_side_effects=True, vmem_limit_bytes=56 * 1024 * 1024),
    )
    results = call(
        features, weight, bias.reshape(1, HID),
        adj_tiles.reshape(BLOCKS * SHARDS, 2, EDGE, EDGE), adj_cols.transpose(0, 2, 1), degree, grad_out)
    act, fgrad, wgrad, bgrad = pl.pallas_call(
        hand_over,
        out_shape=outs,
        in_specs=[anywhere] * 4,
        out_specs=(anywhere,) * 4,
        scratch_shapes=[pltpu.VMEM(out.shape, out.dtype) for out in outs] + [pltpu.SemaphoreType.DMA((8,))],
    )(*results)
    return act, fgrad, wgrad, bgrad.reshape(HID)


def solution(mesh):
    return jax.shard_map(
        body,
        mesh=mesh,
        in_specs=(
            P(("dom", "rep"), None),
            P(),
            P(),
            P("dom", None, "rep", None, None),
            P("dom", None, "rep"),
            P("dom", None),
            P(("dom", "rep"), None),
        ),
        out_specs=(P(("dom", "rep"), None), P(("dom", "rep"), None), P(), P()),
        check_vma=False,
    )
```

time: 613 us -> 117 us (0.19)
  waiting for transfers between devices: 314 us -> 0 us
  blocking collectives: 147 us -> 0 us
  Pallas kernels: 0 us -> 116 us
  matrix products: 60 us -> 0 us
  other arithmetic: 39.1 us -> 0 us
  local copies, waits for them, and re-layouts: 30.1 us -> 0 us
  between operations: 13.9 us -> 0.64 us
    pallas_call x0 -> x2, Pallas kernels: none -> 116 us  [the longest x1 114 us: body(): call(features, weight, bias.reshape(1, HID), adj_tiles.reshape(BLOCKS * S...]
    all_gather x2 -> x0, waiting for transfers between devices: 116 us -> none  [the longest x1 85.9 us: body(): arrived = lax.all_gather(shard_features, 'dom', axis=0, tiled=True)]
    all_to_all x1 -> x0, waiting for transfers between devices: 95.5 us -> none  [body(): lax.all_to_all(tile_vals, 'dom', split_axis=1, concat_axis=1, tiled=True)]
    reduce_scatter x2 -> x0, waiting for transfers between devices: 80.6 us -> none  [the longest x1 42.5 us: body(): lax.psum_scatter(partial_value.reshape(shard_rows, hidden), 'rep', scatte...]
    all_gather x2 -> x0, blocking collectives: 67.9 us -> none  [the longest x1 34.7 us: body(): shard_features = lax.all_gather(features, 'rep', axis=0, tiled=True)]
    psum x1 -> x0, blocking collectives: 65.6 us -> none  [body(): weight_sum, bias_sum = lax.psum((weight_term, bias_term), ('dom', 'rep'))]
    dot_general x35 -> x0, matrix products: 60 us -> none  [the longest x16 30.1 us: gather_add_shard(): jnp.einsum('bkxy,bkyf->bxf', part_tiles, selected, preferred_element_type...]
    scatter-add x16 -> x0, other arithmetic: 29.5 us -> none  [back_add_shard(): return inner.at[part_cols].add(product)]
  transfers between devices with their start and end apart: 6 -> 0, of which waited for: 6 -> 0; matrix products, arithmetic and copies ran while one was open for 11% -> 0% of each run, Pallas kernels for 0% -> 0%
where the time goes in v2:
time: 117 us
  Pallas kernels  116 us (99%)
    pallas_call x1, Pallas kernels, body(): call(features, weight, bias.reshape(1, HID), adj_tiles.reshape(BLOCKS * S...  114 us

profile of v2, /device:TPU:0, one launch (start us, length us, event | category | flops | bytes accessed | tf_op | source)
XLA Modules:
  0.0 117.0 jit_solution(16100707059179021227)
XLA Ops:
  0.6 114.5 %shard_map.102 = (bf16[192,256]{1,0:T(8,128)(2,1)}, bf16[192,256]{1,0:T(8,128)(2,1)}, f32[256,256]{1,0:T(8,128)}, f32[1,256]{1,0:T(1,128)}) custom-call(bf16[192,256]{1,0:T(8,128)(2,1)} %refs_0_.1, bf16[256,256]{1,0:T(8,128)(2,1)} %refs_1_.1, f32[1,256]{1,0:T(1,128)} %bitcast.6, bf16[96,2,128,128]{3,2,1,0:T(8,128)(2,1)} %bitcast.4, s32[12,1,16]{2,1,0:T(1,128)} %bitcast.5, ...), custom_call_target="tpu_custom_call" | custom-call | tf_op jit(solution)/shard_map/pallas_call | solution.py:594
  115.1 1.8 %shard_map.103 = (bf16[192,256]{1,0:T(8,128)(2,1)}, bf16[192,256]{1,0:T(8,128)(2,1)}, f32[256,256]{1,0:T(8,128)}, f32[1,256]{1,0:T(1,128)}) custom-call(bf16[192,256]{1,0:T(8,128)(2,1)} %get-tuple-element.12.refs_0_, bf16[192,256]{1,0:T(8,128)(2,1)} %get-tuple-element.13.refs_1_, f32[256,256]{1,0:T(8,128)} %get-tuple-element.14.refs_2_, ...), custom_call_target="tpu_custom_call" | custom-call | tf_op jit(solution)/shard_map/pallas_call | solution.py:597

commit v3 on v2

v3 whole, which is shorter than its diff:
```python
import math

import jax
import jax.numpy as jnp
from jax import lax
from jax.experimental import pallas as pl
from jax.experimental.pallas import tpu as pltpu
from jax.sharding import PartitionSpec as P

MESH = pl.DeviceIdType.MESH
BF16, F32, I32 = jnp.bfloat16, jnp.float32, jnp.int32
RING, SIDE = 4, 64
BLOCKS, SHARDS, EDGE, HID = 12, 8, 128, 256
CHUNK = 192
REPS = 8
NONE = BLOCKS
EMPTY = 192
ROOT = math.sqrt(2.0 / math.pi)
CUBIC = 0.044715


def wrap(value, size):
    return lax.rem(value, size)


def turned(part, x, y, z):
    at = (x, y, z)
    return at[(part + 2) % 3], at[(part + 1) % 3], at[part]


def place(part, x, y, z):
    c, b, a = turned(part, x, y, z)
    return part * 64 + c * 16 + b * 4 + a


def kernel(scale, feat, weight_in, bias_in, tiles, cols_in, degree_in, grad_in,
           act_out, fgrad_out, wgrad_out, bgrad_out,
           weight, bias, cols, degree, grad, act, fgrad,
           swapped, flipped, table_own, table_in, table, gathered,
           theirs, arrived, mine, shares, landed, spread,
           chain_own, chain, grads, land_r, land_y, land_row, land_piece,
           wterm, wx, wcore_out, wcore, whi_out, whi, wrep, wall, bsum_out,
           sems):
    dom, rep = lax.axis_index("dom"), lax.axis_index("rep")
    core = wrap(dom, 2)
    x = wrap(lax.div(dom, 2), 4)
    y_hi = lax.div(dom, 8)
    z, y_lo = lax.div(rep, 2), wrap(rep, 2)
    y = y_hi * 2 + y_lo
    at = (x, y, z)

    def near(axis, step):
        to = list(at)
        to[axis] = wrap(at[axis] + step, RING)
        return (lax.div(to[1], 2) * 4 + to[0]) * 2 + core, to[2] * 2 + wrap(to[1], 2)

    def peer(k):
        return dom, wrap(rep + k, REPS)

    partner = (dom + 1 - 2 * core, rep)
    across = (wrap(dom + 8, 16), rep)

    barrier = pltpu.get_barrier_semaphore()

    def greet(target):
        pl.semaphore_signal(barrier, inc=1, device_id=target, device_id_type=MESH)

    for axis in range(3):
        for step in (1, 3, 2):
            greet(near(axis, step))
    greet(partner)
    for k in range(1, REPS):
        greet(peer(k))

    used = [0]
    started = []

    def lane(count=1):
        used[0] += count
        return used[0] - count

    def local(src, dst):
        copy = pltpu.make_async_copy(src, dst, sems.at[lane()])
        copy.start()
        return copy

    def remote(src, dst, target, slot=None):
        slot = lane(2) if slot is None else slot
        return pltpu.make_async_remote_copy(
            src_ref=src, dst_ref=dst, send_sem=sems.at[slot], recv_sem=sems.at[slot + 1],
            device_id=target, device_id_type=MESH)

    def send(src, dst, target, slot=None):
        copy = remote(src, dst, target, slot)
        copy.start()
        started.append(copy)
        return copy

    small = [local(cols_in, cols), local(degree_in, degree)]
    pieces = [local(feat.at[pl.ds(part * SIDE, SIDE)], gathered.at[place(part, x, y, z)]) for part in range(3)]
    own_tiles = local(tiles.at[:, core], swapped.at[0])
    dense_in = [local(weight_in, weight), local(bias_in, bias), local(grad_in, grad)]
    gathered[EMPTY] = jnp.zeros((SIDE, HID), BF16)

    pl.semaphore_wait(barrier, 9 + 1 + REPS - 1)

    def row_of(part, c, b):
        return gathered.at[pl.ds(part * 64 + c * 16 + b * 4, 4)]

    def half_of(part, b, h):
        return gathered.at[pl.ds(part * 64 + at[(part + 2) % 3] * 16 + b * 4 + 2 * h, 2)]

    first = []
    for part in range(3):
        for step in (1, 3, 2):
            first.append(send(feat.at[pl.ds(part * SIDE, SIDE)], gathered.at[place(part, x, y, z)], near(part, step)))
    tile_copy = send(tiles.at[:, 1 - core], swapped.at[1], partner)

    def flip(which, b0, count):
        def body(b, carry):
            for s in range(SHARDS):
                spot = (s % 4) * 2 + s // 4
                flipped[which, b, pl.ds(spot * EDGE, EDGE), :] = jnp.transpose(swapped[which, b * SHARDS + s])
            return carry
        lax.fori_loop(b0, b0 + count, body, 0)

    for copy in pieces:
        copy.wait()
    for copy in first:
        copy.wait_recv()

    slots_1 = [[[lane(2) for k in range(3)] for way in range(2)] for part in range(3)]
    slots_2 = [[[lane(2) for k in range(6)] for way in range(2)] for part in range(3)]
    FIRST, SECOND = (0, 1), (3, 2)

    def ways():
        for part in range(3):
            for way in range(2):
                yield part, way, (1 if way == 0 else 3)

    def round_1(part, way, step, k, go):
        m = at[(part + 1) % 3]
        h = way if k in (0, 2) else 1 - way
        if go:
            b = m if k < 2 else wrap(m + 4 - step, RING)
        else:
            b = wrap(m + (4 - step) * (1 if k < 2 else 2), RING)
        ref = half_of(part, b, h)
        target, slot = near((part + 1) % 3, step), slots_1[part][way][k]
        if go:
            send(ref, ref, target, slot)
        else:
            remote(ref, ref, target, slot).wait_recv()

    def round_2(part, way, step, k, go):
        m, b0 = at[(part + 2) % 3], at[(part + 1) % 3]
        offset = k if k < 4 else (FIRST if way == 0 else SECOND)[k - 4]
        if go:
            c = m if k < 4 else wrap(m + 4 - step, RING)
        else:
            c = wrap(m + (4 - step) * (1 if k < 4 else 2), RING)
        ref = row_of(part, c, wrap(b0 + offset, RING))
        target, slot = near((part + 2) % 3, step), slots_2[part][way][k]
        if go:
            send(ref, ref, target, slot)
        else:
            remote(ref, ref, target, slot).wait_recv()

    def each(action, k, go):
        for part, way, step in ways():
            action(part, way, step, k, go)

    each(round_1, 0, True)
    each(round_1, 1, True)
    each(round_2, 0, True)

    for copy in small:
        copy.wait()
    col = cols[:, 0, :]
    live = rep < degree[...]
    shard = lax.div(lax.broadcasted_iota(I32, (BLOCKS, 16), 1), 2)
    shard_x, shard_y = wrap(shard, 4), lax.div(shard, 4) * 2
    block = lax.broadcasted_iota(I32, (BLOCKS, 16), 0)
    table_own[...] = jnp.zeros(table_own.shape, I32)
    for h in range(2):
        q = 2 * col + h
        r = (q * 11) >> 5
        part, to_z = q - 3 * r, r >> 1
        to_y = shard_y + (r - 2 * to_z)
        spot = jnp.where(part == 0, place(0, shard_x, to_y, to_z),
                         jnp.where(part == 1, place(1, shard_x, to_y, to_z), place(2, shard_x, to_y, to_z)))
        table_own[16 * h:16 * h + BLOCKS, 0:16] = jnp.where(live, spot, EMPTY)
    third = (block * 11) >> 5
    turn_of = wrap(third + 4 - z, RING)
    rank = jnp.where(turn_of == 0, 0, jnp.where(turn_of == 3, 3, jnp.where(turn_of == 1, 6, 9))) + block - 3 * third
    before = jnp.full((BLOCKS, 16), -1, I32)
    last = jnp.full((BLOCKS, 16), -1, I32)
    for b in range(BLOCKS):
        here, spot = live[b:b + 1], rank[b:b + 1]
        before = jnp.where((col == col[b:b + 1]) & here & (spot < rank), jnp.maximum(before, spot), before)
        last = jnp.where((block == col[b:b + 1]) & here, jnp.maximum(last, spot), last)
    table_own[32:32 + BLOCKS, 0:16] = jnp.where(before < 0, NONE, before)
    table_own[48:48 + BLOCKS, 0:16] = jnp.where(last < 0, NONE, last)
    table_copy = send(table_own, table_in, partner)
    own_table = local(table_own, table.at[0])

    own_tiles.wait()
    flip(0, 0, 1)
    each(round_1, 0, False)
    each(round_1, 2, True)
    each(round_1, 1, False)
    each(round_2, 1, True)
    each(round_2, 3, True)
    flip(0, 1, 1)
    each(round_2, 0, False)
    for part, way, step in ways():
        if way == 0:
            round_2(part, way, step, 4, True)
    each(round_1, 2, False)
    each(round_2, 2, True)
    flip(0, 2, 4)
    each(round_2, 1, False)
    each(round_2, 3, False)
    for part, way, step in ways():
        if way == 0:
            round_2(part, way, step, 5, True)
        else:
            round_2(part, way, step, 4, True)
    flip(0, 6, 6)
    own_table.wait()
    table_copy.wait_recv()
    their_table = local(table_in, table.at[1])
    tile_copy.wait_recv()
    each(round_2, 2, False)
    for part, way, step in ways():
        if way == 1:
            round_2(part, way, step, 5, True)
    flip(1, 0, 12)
    their_table.wait()
    each(round_2, 4, False)
    each(round_2, 5, False)

    def entry(which, kind, b, s):
        return table[which, kind * 16 + b, 2 * s + core]

    def row_block(which, b):
        lhs = jnp.concatenate([swapped[which, b * SHARDS + s] for s in range(SHARDS)], axis=1)
        rhs = jnp.concatenate([gathered[entry(which, h, b, s)] for s in range(SHARDS) for h in range(2)], axis=0)
        return jnp.dot(lhs, rhs, preferred_element_type=F32)

    def rows_of(r):
        return pl.ds(pl.multiple_of(r * CHUNK, CHUNK), CHUNK)

    def edge_of(b):
        return pl.ds(pl.multiple_of(b * EDGE, EDGE), EDGE)

    def their_block(b, carry):
        theirs[edge_of(b), :] = row_block(1, b).astype(BF16)
        return carry

    def my_block(b, carry):
        mine[edge_of(b), :] = row_block(0, b)
        return carry

    def beside(dz, dy):
        return wrap(z + dz, RING) * 2 + wrap(y_lo + dy, 2)

    def share(dz, dy):
        to = beside(dz, dy)
        rows = rows_of(to)
        shares[to] = (mine[rows, :] + arrived[rows, :].astype(F32)).astype(BF16)
        return send(shares.at[to], landed.at[rep], (dom, to))

    swap, slots = [], []
    order = (2, 1, 3, 0)
    for g in range(4):
        base = wrap(z + order[g], RING)
        lax.fori_loop(base * 3, base * 3 + 3, their_block, 0)
        rows = pl.ds(pl.multiple_of(base * 384, 384), 384)
        swap.append(send(theirs.at[rows], arrived.at[rows], partner))
        if g:
            swap[g - 1].wait_recv()
            for dy in (1, 0):
                slots.append((order[g - 1], dy, share(order[g - 1], dy)))
        lax.fori_loop(base * 3, base * 3 + 3, my_block, 0)
    swap[3].wait_recv()
    slots.append((0, 1, share(0, 1)))

    total = mine[rows_of(rep), :] + arrived[rows_of(rep), :].astype(F32)
    for copy in dense_in:
        copy.wait()
    for dz, dy, copy in slots:
        copy.wait_recv()
        total = total + landed[beside(4 - dz, dy)].astype(F32)

    aggregated = total.astype(BF16)
    v = jnp.dot(aggregated, weight[...], preferred_element_type=F32) + bias[...]
    t = jnp.tanh(ROOT * (v + CUBIC * (v * v * v)))
    slope = 0.5 * (1.0 + t) + 0.5 * v * ((1.0 - t) * (1.0 + t)) * (ROOT * (1.0 + 3.0 * CUBIC * (v * v)))
    delta = (grad[...].astype(F32) * slope).astype(BF16)
    spread[0, rows_of(rep), :] = lax.dot_general(
        delta, weight[...], (((1,), (1,)), ((), ())), preferred_element_type=F32).astype(BF16)
    here = spread.at[0, rows_of(rep)]
    spread_in = {}
    for dz in (0, 1, 3, 2):
        for dy in (0, 1):
            if dz or dy:
                spread_in[dz, dy] = send(here, here, (dom, beside(dz, dy)))
    forward_in = [send(here, spread.at[1, rows_of(rep)], partner)]
    act[...] = (0.5 * v * (1.0 + t)).astype(BF16)
    outgoing = [local(act, act_out)]

    wsum = lax.dot_general(aggregated, delta, (((0,), (0,)), ((), ())), preferred_element_type=F32)
    bsum = jnp.sum(delta.astype(F32).reshape(CHUNK // 8, 8, HID), axis=0)
    for k in range(RING):
        wterm[k, 0:64, :] = wsum[k * 64:(k + 1) * 64, :]
        wterm[k, 64:72, :] = bsum
    wx[x] = wterm[x]
    w_x = [send(wterm.at[wrap(x + k, RING)], wx.at[x], near(0, k)) for k in range(1, RING)]

    for s in range(SHARDS):
        chain_own[s, NONE] = jnp.zeros((EDGE, HID), F32)
    for s in range(2):
        chain[s, NONE] = jnp.zeros((EDGE, HID), F32)

    for turn_at in range(4):
        dz = (0, 1, 3, 2)[turn_at]
        for dy in (0, 1):
            if dz or dy:
                spread_in[dz, dy].wait_recv()
                rows = rows_of(beside(4 - dz, dy))
                forward_in.append(send(spread.at[0, rows], spread.at[1, rows], partner))
        base = wrap(z + 4 - dz, RING) * 3

        def own_block(j, carry):
            b = base + j
            source = spread[0, edge_of(b), :]
            for to_x in range(4):
                product = jnp.dot(flipped[0, b, pl.ds(to_x * 2 * EDGE, 2 * EDGE), :], source, preferred_element_type=F32)
                for s in range(2):
                    prior = chain_own[to_x * 2 + s, entry(0, 2, b, s * 4 + to_x)]
                    chain_own[to_x * 2 + s, turn_at * 3 + j] = product[s * EDGE:(s + 1) * EDGE] + prior
            return carry
        lax.fori_loop(0, 3, own_block, 0)

    def link(to_x):
        rows = pl.ds(pl.multiple_of(to_x * 2 * EDGE, 2 * EDGE), 2 * EDGE)
        for turn_at in range(4):
            base = wrap(z + (0, 3, 1, 2)[turn_at], RING) * 3
            blocks = [base + j for j in range(3)]
            products = [
                jnp.dot(flipped[1, b, rows, :], spread[1, edge_of(b), :], preferred_element_type=F32) for b in blocks]
            for j, b in enumerate(blocks):
                for s in range(2):
                    prior = chain[s, entry(1, 2, b, s * 4 + to_x)]
                    chain[s, turn_at * 3 + j] = products[j][s * EDGE:(s + 1) * EDGE] + prior

    def close(to_x):
        for s in range(2):
            for c in range(BLOCKS):
                both = (chain_own[to_x * 2 + s, entry(0, 3, c, s * 4 + to_x)]
                        + chain[s, entry(1, 3, c, s * 4 + to_x)]).astype(BF16)
                for h in range(2):
                    q = 2 * c + h
                    part, r = q % 3, q // 3
                    grads[(part,) + turned(part, to_x, s * 2 + r % 2, r // 2)] = both[h * SIDE:(h + 1) * SIDE]

    off = (2, 1, 3, 0)
    to_xs = [wrap(x + d, RING) for d in off]
    to_zs = [wrap(z + d, RING) for d in off]
    slots_r = [[[[lane(2) for k in range(3)] for way in range(2)] for g in range(4)] for part in range(3)]
    ring_of = (2, 0, 1)

    def quarter(part, plane, g, h):
        if part == 0:
            return grads.at[0, plane, pl.ds(2 * h, 2), to_xs[g]]
        return grads.at[part, plane, (to_zs if part == 1 else to_xs)[g], pl.ds(2 * h, 2)]

    def land_of(part, g, way, k):
        return land_r.at[((part * 4 + g) * 2 + way) * 3 + k]

    def quarter_copy(part, g, way, k):
        axis, step = ring_of[part], (1, 3)[way]
        plane = wrap(at[axis] + (2 if k == 0 else step), RING)
        h = way if k in (0, 2) else 1 - way
        return remote(quarter(part, plane, g, h), land_of(part, g, way, k), near(axis, step), slots_r[part][g][way][k])

    def begin(copy):
        copy.start()
        started.append(copy)

    def begin_each(parts, g, k):
        for part in parts:
            for way in range(2):
                begin(quarter_copy(part, g, way, k))

    def add_to(ref, *others):
        full = ref[...].astype(F32)
        for other in others:
            full = full + other[...].astype(F32)
        ref[...] = full.astype(BF16)

    def pass_on(g):
        for part in range(3):
            for way in range(2):
                quarter_copy(part, g, way, 0).wait_recv()
                plane = wrap(at[ring_of[part]] + (1, 3)[way], RING)
                add_to(quarter(part, plane, g, way), land_of(part, g, way, 0))
                begin(quarter_copy(part, g, way, 2))

    rows_sent = {}

    def settle(g):
        for part in range(3):
            for way in range(2):
                for k in (1, 2):
                    quarter_copy(part, g, way, k).wait_recv()
            plane = at[ring_of[part]]
            for h in range(2):
                add_to(quarter(part, plane, g, h), land_of(part, g, h, 2), land_of(part, g, 1 - h, 1))
            if part == 0:
                for k in range(1, RING):
                    rows_sent[0, g, k] = send(
                        grads.at[0, z, wrap(y + k, RING), to_xs[g]], land_y.at[g * 3 + k - 1], near(1, k))
            elif g < 3:
                row = (to_zs if part == 1 else to_xs)[g]
                rows_sent[part, g] = send(
                    grads.at[part, plane, row], land_row.at[(part - 1) * 3 + g], near((2, 0)[part - 1], off[g]))

    pieces_sent = {}

    def column_in(g):
        for k in range(1, RING):
            rows_sent[0, g, k].wait_recv()
        piece = grads.at[0, z, y, to_xs[g]]
        add_to(piece, *[land_y.at[g * 3 + k] for k in range(3)])
        if g < 3:
            pieces_sent[0, g] = send(piece, land_piece.at[g], near(0, off[g]))

    def row_in(part):
        for g in range(3):
            rows_sent[part, g].wait_recv()
        plane, row = (x, z) if part == 1 else (y, x)
        add_to(grads.at[part, plane, row], *[land_row.at[(part - 1) * 3 + g] for g in range(3)])
        axis = (1, 2)[part - 1]
        for g in range(3):
            pieces_sent[part, g] = send(grads.at[part, plane, row, wrap(at[axis] + off[g], RING)],
                                        land_piece.at[part * 3 + g], near(axis, off[g]))

    def piece_in(part):
        plane, row, spot = turned(part, x, y, z)
        full = grads[part, plane, row, spot].astype(F32)
        for g in range(3):
            pieces_sent[part, g].wait_recv()
            full = full + land_piece[part * 3 + g].astype(F32)
        fgrad[pl.ds(part * SIDE, SIDE), :] = full.astype(BF16)

    for copy in forward_in:
        copy.wait_recv()
    for g in range(4):
        link(to_xs[g])
        close(to_xs[g])
        begin_each((0, 2), g, 0)
        if g == 0:
            for q in range(4):
                begin_each((1,), q, 0)

    for copy in w_x:
        copy.wait_recv()
    wx[0] = wx[0] + wx[1] + wx[2] + wx[3]
    wcore_out[0:32, :] = wx[0, pl.ds(pl.multiple_of((1 - core) * 32, 32), 32), :]
    wcore_out[32:40, :] = wx[0, 64:72, :]
    w_core = send(wcore_out, wcore, partner)

    begin_each(range(3), 0, 1)
    pass_on(0)
    w_core.wait_recv()
    wcore[0:32, :] = wcore[0:32, :] + wx[0, pl.ds(pl.multiple_of(core * 32, 32), 32), :]
    wcore[32:40, :] = wcore[32:40, :] + wx[0, 64:72, :]
    whi_out[0:16, :] = wcore[pl.ds(pl.multiple_of((1 - y_hi) * 16, 16), 16), :]
    whi_out[16:24, :] = wcore[32:40, :]
    w_hi = send(whi_out, whi, across)

    begin_each(range(3), 1, 1)
    pass_on(1)
    w_hi.wait_recv()
    wrep[rep, 0:16, :] = whi[0:16, :] + wcore[pl.ds(pl.multiple_of(y_hi * 16, 16), 16), :]
    wrep[rep, 16:24, :] = whi[16:24, :] + wcore[32:40, :]
    w_rep = [send(wrep.at[rep], wrep.at[rep], peer(k)) for k in range(1, REPS)]

    begin_each(range(3), 2, 1)
    pass_on(2)
    settle(0)
    for copy in w_rep:
        copy.wait_recv()
    wfull = wrep[0]
    for r in range(1, REPS):
        wfull = wfull + wrep[r]
    wfull = wfull * scale
    bsum_out[...] = jnp.sum(wfull[16:24], axis=0, keepdims=True)
    outgoing.append(local(bsum_out, bgrad_out))

    def wrows(start, count):
        return wall.at[pl.ds(pl.multiple_of(start, 16), count)]

    wall[pl.ds(pl.multiple_of(x * 64 + core * 32 + y_hi * 16, 16), 16), :] = wfull[0:16]
    ref = wrows(x * 64 + core * 32 + y_hi * 16, 16)
    w_hi = send(ref, ref, across)

    begin_each(range(3), 3, 1)
    pass_on(3)
    settle(1)
    w_hi.wait_recv()
    ref = wrows(x * 64 + core * 32, 32)
    w_core = send(ref, ref, partner)
    column_in(0)
    settle(2)
    w_core.wait_recv()
    ref = wrows(x * 64, 64)
    w_x = [send(ref, ref, near(0, k)) for k in range(1, RING)]
    column_in(1)
    settle(3)
    row_in(1)
    row_in(2)
    column_in(2)
    for copy in w_x:
        copy.wait_recv()
    outgoing.append(local(wall, wgrad_out))
    column_in(3)
    for part in (0, 1, 2):
        piece_in(part)
    outgoing.append(local(fgrad, fgrad_out))
    for copy in started:
        copy.wait_send()
    for copy in outgoing:
        copy.wait()


def hand_over(*refs):
    ins, outs, held, sems = refs[:4], refs[4:8], refs[8:12], refs[12]
    copies = [pltpu.make_async_copy(ins[k], held[k], sems.at[k]) for k in range(4)]
    for copy in copies:
        copy.start()
    onward = []
    for k in range(4):
        copies[k].wait()
        onward.append(pltpu.make_async_copy(held[k], outs[k], sems.at[4 + k]))
        onward[k].start()
    for copy in onward:
        copy.wait()


def body(features, weight, bias, adj_tiles, adj_cols, degree, grad_out):
    anywhere = pl.BlockSpec(memory_space=pl.ANY)
    rows = BLOCKS * EDGE
    scale = 1.0 / math.sqrt(CHUNK * REPS * 16)
    outs = (
        jax.ShapeDtypeStruct((CHUNK, HID), BF16),
        jax.ShapeDtypeStruct((CHUNK, HID), BF16),
        jax.ShapeDtypeStruct((HID, HID), F32),
        jax.ShapeDtypeStruct((1, HID), F32),
    )
    call = pl.pallas_call(
        lambda *refs: kernel(scale, *refs),
        out_shape=outs,
        in_specs=[anywhere] * 7,
        out_specs=(anywhere,) * 4,
        scratch_shapes=[
            pltpu.VMEM((HID, HID), BF16),
            pltpu.VMEM((1, HID), F32),
            pltpu.VMEM((BLOCKS, 1, 16), I32),
            pltpu.VMEM((BLOCKS, 16), I32),
            pltpu.VMEM((CHUNK, HID), BF16),
            pltpu.VMEM((CHUNK, HID), BF16),
            pltpu.VMEM((CHUNK, HID), BF16),
            pltpu.VMEM((2, BLOCKS * SHARDS, EDGE, EDGE), BF16),
            pltpu.VMEM((2, BLOCKS, SHARDS * EDGE, EDGE), BF16),
            pltpu.VMEM((64, 128), I32),
            pltpu.VMEM((64, 128), I32),
            pltpu.SMEM((2, 64, 128), I32),
            pltpu.VMEM((193, SIDE, HID), BF16),
            pltpu.VMEM((rows, HID), BF16),
            pltpu.VMEM((rows, HID), BF16),
            pltpu.VMEM((rows, HID), F32),
            pltpu.VMEM((REPS, CHUNK, HID), BF16),
            pltpu.VMEM((REPS, CHUNK, HID), BF16),
            pltpu.VMEM((2, rows, HID), BF16),
            pltpu.VMEM((SHARDS, 13, EDGE, HID), F32),
            pltpu.VMEM((2, 13, EDGE, HID), F32),
            pltpu.VMEM((3, 4, 4, 4, SIDE, HID), BF16),
            pltpu.VMEM((72, 2, SIDE, HID), BF16),
            pltpu.VMEM((12, SIDE, HID), BF16),
            pltpu.VMEM((6, 4, SIDE, HID), BF16),
            pltpu.VMEM((9, SIDE, HID), BF16),
            pltpu.VMEM((RING, 72, HID), F32),
            pltpu.VMEM((RING, 72, HID), F32),
            pltpu.VMEM((40, HID), F32),
            pltpu.VMEM((40, HID), F32),
            pltpu.VMEM((24, HID), F32),
            pltpu.VMEM((24, HID), F32),
            pltpu.VMEM((REPS, 24, HID), F32),
            pltpu.VMEM((HID, HID), F32),
            pltpu.VMEM((1, HID), F32),
            pltpu.SemaphoreType.DMA((512,)),
        ],
        compiler_params=pltpu.CompilerParams(
            collective_id=0, has_side_effects=True, vmem_limit_bytes=61 * 1024 * 1024),
    )
    results = call(
        features, weight, bias.reshape(1, HID),
        adj_tiles.reshape(BLOCKS * SHARDS, 2, EDGE, EDGE), adj_cols.transpose(0, 2, 1), degree, grad_out)
    act, fgrad, wgrad, bgrad = pl.pallas_call(
        hand_over,
        out_shape=outs,
        in_specs=[anywhere] * 4,
        out_specs=(anywhere,) * 4,
        scratch_shapes=[pltpu.VMEM(out.shape, out.dtype) for out in outs] + [pltpu.SemaphoreType.DMA((8,))],
    )(*results)
    return act, fgrad, wgrad, bgrad.reshape(HID)


def solution(mesh):
    return jax.shard_map(
        body,
        mesh=mesh,
        in_specs=(
            P(("dom", "rep"), None),
            P(),
            P(),
            P("dom", None, "rep", None, None),
            P("dom", None, "rep"),
            P("dom", None),
            P(("dom", "rep"), None),
        ),
        out_specs=(P(("dom", "rep"), None), P(("dom", "rep"), None), P(), P()),
        check_vma=False,
    )
```

time: 117 us -> 105 us (0.90)
  Pallas kernels: 116 us -> 104 us
    pallas_call x1, Pallas kernels: 114 us -> 102 us  [body(): call(features, weight, bias.reshape(1, HID), adj_tiles.reshape(BLOCKS * S...]
where the time goes in v3:
time: 105 us; the launch traced here: 104 us
  Pallas kernels  104 us (99%)
    pallas_call x1, Pallas kernels, body(): call(features, weight, bias.reshape(1, HID), adj_tiles.reshape(BLOCKS * S...  102 us

profile of v3, /device:TPU:0, one launch (start us, length us, event | category | flops | bytes accessed | tf_op | source)
XLA Modules:
  0.0 104.3 jit_solution(1756540600306363196)
XLA Ops:
  0.6 101.8 %shard_map.102 = (bf16[192,256]{1,0:T(8,128)(2,1)}, bf16[192,256]{1,0:T(8,128)(2,1)}, f32[256,256]{1,0:T(8,128)}, f32[1,256]{1,0:T(1,128)}) custom-call(bf16[192,256]{1,0:T(8,128)(2,1)} %refs_0_.1, bf16[256,256]{1,0:T(8,128)(2,1)} %refs_1_.1, f32[1,256]{1,0:T(1,128)} %bitcast.6, bf16[96,2,128,128]{3,2,1,0:T(8,128)(2,1)} %bitcast.4, s32[12,1,16]{2,1,0:T(1,128)} %bitcast.5, ...), custom_call_target="tpu_custom_call" | custom-call | tf_op jit(solution)/shard_map/pallas_call | solution.py:609
  102.4 1.8 %shard_map.103 = (bf16[192,256]{1,0:T(8,128)(2,1)}, bf16[192,256]{1,0:T(8,128)(2,1)}, f32[256,256]{1,0:T(8,128)}, f32[1,256]{1,0:T(1,128)}) custom-call(bf16[192,256]{1,0:T(8,128)(2,1)} %get-tuple-element.12.refs_0_, bf16[192,256]{1,0:T(8,128)(2,1)} %get-tuple-element.13.refs_1_, f32[256,256]{1,0:T(8,128)} %get-tuple-element.14.refs_2_, ...), custom_call_target="tpu_custom_call" | custom-call | tf_op jit(solution)/shard_map/pallas_call | solution.py:612

commit v4 on v3

--- a/solution.py
+++ b/solution.py
@@ -104,16 +104,52 @@
 
     pl.semaphore_wait(barrier, 9 + 1 + REPS - 1)
 
-    def row_of(part, c, b):
-        return gathered.at[pl.ds(part * 64 + c * 16 + b * 4, 4)]
-
-    def half_of(part, b, h):
-        return gathered.at[pl.ds(part * 64 + at[(part + 2) % 3] * 16 + b * 4 + 2 * h, 2)]
-
-    first = []
+    def piece_of(part, c, b, a):
+        return gathered.at[part * 64 + c * 16 + b * 4 + a]
+
+    def move(part, axis, way, ref, slot, go):
+        copy = remote(ref, ref, near(axis, (1, 3)[way]), slot)
+        if go:
+            copy.start()
+            started.append(copy)
+        else:
+            copy.wait_recv()
+
+    def from_where(m, way, passed, go):
+        return wrap(m + (passed + (0 if go else 1)) * (4 - (1, 3)[way]), RING)
+
+    slots_1 = [[[lane(2) for k in range(8)] for way in range(2)] for part in range(3)]
+    slots_2 = [[[lane(2) for k in range(12)] for way in range(2)] for part in range(3)]
+
+    def round_1(way, o, passed, go, parts=(0, 1, 2)):
+        for part in parts:
+            b = from_where(at[(part + 1) % 3], way, passed, go)
+            ref = piece_of(part, at[(part + 2) % 3], b, wrap(at[part] + o, RING))
+            move(part, (part + 1) % 3, way, ref, slots_1[part][way][4 * passed + o], go)
+
+    def round_2(way, o, go, parts=(0, 1, 2)):
+        for part in parts:
+            c = from_where(at[(part + 2) % 3], way, 0, go)
+            ref = piece_of(part, c, at[(part + 1) % 3], wrap(at[part] + o, RING))
+            move(part, (part + 2) % 3, way, ref, slots_2[part][way][o], go)
+
+    def round_3(way, row, passed, go):
+        for part in range(3):
+            c = from_where(at[(part + 2) % 3], way, passed, go)
+            b = wrap(at[(part + 1) % 3] + row, RING)
+            ref = gathered.at[pl.ds(part * 64 + c * 16 + b * 4, 4)]
+            move(part, (part + 2) % 3, way, ref, slots_2[part][way][4 + 4 * passed + row], go)
+
+    for copy in pieces:
+        copy.wait()
+    first = {}
     for part in range(3):
-        for step in (1, 3, 2):
-            first.append(send(feat.at[pl.ds(part * SIDE, SIDE)], gathered.at[place(part, x, y, z)], near(part, step)))
+        own = gathered.at[place(part, x, y, z)]
+        for o in (3, 1, 2):
+            first[part, o] = send(own, own, near(part, 4 - o))
+    for way in range(2):
+        round_1(way, 0, 0, True)
+        round_2(way, 0, True)
     tile_copy = send(tiles.at[:, 1 - core], swapped.at[1], partner)
 
     def flip(which, b0, count):
@@ -123,56 +159,6 @@
                 flipped[which, b, pl.ds(spot * EDGE, EDGE), :] = jnp.transpose(swapped[which, b * SHARDS + s])
             return carry
         lax.fori_loop(b0, b0 + count, body, 0)
-
-    for copy in pieces:
-        copy.wait()
-    for copy in first:
-        copy.wait_recv()
-
-    slots_1 = [[[lane(2) for k in range(3)] for way in range(2)] for part in range(3)]
-    slots_2 = [[[lane(2) for k in range(6)] for way in range(2)] for part in range(3)]
-    FIRST, SECOND = (0, 1), (3, 2)
-
-    def ways():
-        for part in range(3):
-            for way in range(2):
-                yield part, way, (1 if way == 0 else 3)
-
-    def round_1(part, way, step, k, go):
-        m = at[(part + 1) % 3]
-        h = way if k in (0, 2) else 1 - way
-        if go:
-            b = m if k < 2 else wrap(m + 4 - step, RING)
-        else:
-            b = wrap(m + (4 - step) * (1 if k < 2 else 2), RING)
-        ref = half_of(part, b, h)
-        target, slot = near((part + 1) % 3, step), slots_1[part][way][k]
-        if go:
-            send(ref, ref, target, slot)
-        else:
-            remote(ref, ref, target, slot).wait_recv()
-
-    def round_2(part, way, step, k, go):
-        m, b0 = at[(part + 2) % 3], at[(part + 1) % 3]
-        offset = k if k < 4 else (FIRST if way == 0 else SECOND)[k - 4]
-        if go:
-            c = m if k < 4 else wrap(m + 4 - step, RING)
-        else:
-            c = wrap(m + (4 - step) * (1 if k < 4 else 2), RING)
-        ref = row_of(part, c, wrap(b0 + offset, RING))
-        target, slot = near((part + 2) % 3, step), slots_2[part][way][k]
-        if go:
-            send(ref, ref, target, slot)
-        else:
-            remote(ref, ref, target, slot).wait_recv()
-
-    def each(action, k, go):
-        for part, way, step in ways():
-            action(part, way, step, k, go)
-
-    each(round_1, 0, True)
-    each(round_1, 1, True)
-    each(round_2, 0, True)
 
     for copy in small:
         copy.wait()
@@ -204,41 +190,61 @@
     table_copy = send(table_own, table_in, partner)
     own_table = local(table_own, table.at[0])
 
+    for o in (3, 1, 2):
+        for part in range(3):
+            first[part, o].wait_recv()
+            for way in range(2):
+                round_1(way, o, 0, True, (part,))
+                round_2(way, o, True, (part,))
+    round_1(0, 0, 0, False)
+    round_1(0, 0, 1, True)
+    round_1(1, 0, 0, False)
     own_tiles.wait()
     flip(0, 0, 1)
-    each(round_1, 0, False)
-    each(round_1, 2, True)
-    each(round_1, 1, False)
-    each(round_2, 1, True)
-    each(round_2, 3, True)
-    flip(0, 1, 1)
-    each(round_2, 0, False)
-    for part, way, step in ways():
-        if way == 0:
-            round_2(part, way, step, 4, True)
-    each(round_1, 2, False)
-    each(round_2, 2, True)
-    flip(0, 2, 4)
-    each(round_2, 1, False)
-    each(round_2, 3, False)
-    for part, way, step in ways():
-        if way == 0:
-            round_2(part, way, step, 5, True)
-        else:
-            round_2(part, way, step, 4, True)
-    flip(0, 6, 6)
+    round_1(1, 3, 0, False)
+    round_1(1, 3, 1, True)
+    round_1(0, 3, 0, False)
+    round_1(0, 1, 0, False)
+    round_1(0, 1, 1, True)
+    round_1(1, 1, 0, False)
+    round_1(1, 2, 0, False)
+    round_1(1, 2, 1, True)
+    round_1(0, 2, 0, False)
+    round_3(0, 1, 0, True)
+    round_3(1, 3, 0, True)
+    round_3(0, 3, 0, True)
+    for o in range(4):
+        for way in range(2):
+            round_2(way, o, False)
+    round_3(0, 0, 1, True)
+    for o in (0, 1):
+        round_1(0, o, 1, False)
+    for o in (3, 2):
+        round_1(1, o, 1, False)
+    round_3(1, 2, 0, True)
+    round_3(1, 1, 0, True)
+    round_3(0, 2, 0, True)
+    flip(0, 1, 5)
+    round_3(0, 1, 0, False)
+    round_3(0, 1, 1, True)
+    round_3(1, 3, 0, False)
+    round_3(1, 3, 1, True)
+    flip(0, 6, 4)
+    round_3(1, 2, 0, False)
+    round_3(1, 2, 1, True)
+    flip(0, 10, 2)
     own_table.wait()
     table_copy.wait_recv()
     their_table = local(table_in, table.at[1])
     tile_copy.wait_recv()
-    each(round_2, 2, False)
-    for part, way, step in ways():
-        if way == 1:
-            round_2(part, way, step, 5, True)
     flip(1, 0, 12)
     their_table.wait()
-    each(round_2, 4, False)
-    each(round_2, 5, False)
+    for way, rows in ((0, (3, 2)), (1, (1,))):
+        for row in rows:
+            round_3(way, row, 0, False)
+    for way, rows in ((0, (0, 1)), (1, (3, 2))):
+        for row in rows:
+            round_3(way, row, 1, False)
 
     def entry(which, kind, b, s):
         return table[which, kind * 16 + b, 2 * s + core]
@@ -284,7 +290,11 @@
                 slots.append((order[g - 1], dy, share(order[g - 1], dy)))
         lax.fori_loop(base * 3, base * 3 + 3, my_block, 0)
     swap[3].wait_recv()
+    earlier = started[:-5]
+    del started[:-5]
     slots.append((0, 1, share(0, 1)))
+    for copy in earlier:
+        copy.wait_send()
 
     total = mine[rows_of(rep), :] + arrived[rows_of(rep), :].astype(F32)
     for copy in dense_in:
@@ -342,6 +352,20 @@
                     chain_own[to_x * 2 + s, turn_at * 3 + j] = product[s * EDGE:(s + 1) * EDGE] + prior
             return carry
         lax.fori_loop(0, 3, own_block, 0)
+        if turn_at == 1:
+            for copy in w_x:
+                copy.wait_recv()
+            wx[0] = wx[0] + wx[1] + wx[2] + wx[3]
+            wcore_out[0:32, :] = wx[0, pl.ds(pl.multiple_of((1 - core) * 32, 32), 32), :]
+            wcore_out[32:40, :] = wx[0, 64:72, :]
+            w_core = send(wcore_out, wcore, partner)
+        elif turn_at == 3:
+            w_core.wait_recv()
+            wcore[0:32, :] = wcore[0:32, :] + wx[0, pl.ds(pl.multiple_of(core * 32, 32), 32), :]
+            wcore[32:40, :] = wcore[32:40, :] + wx[0, 64:72, :]
+            whi_out[0:16, :] = wcore[pl.ds(pl.multiple_of((1 - y_hi) * 16, 16), 16), :]
+            whi_out[16:24, :] = wcore[32:40, :]
+            w_hi = send(whi_out, whi, across)
 
     def link(to_x):
         rows = pl.ds(pl.multiple_of(to_x * 2 * EDGE, 2 * EDGE), 2 * EDGE)
@@ -422,8 +446,16 @@
                 for k in range(1, RING):
                     rows_sent[0, g, k] = send(
                         grads.at[0, z, wrap(y + k, RING), to_xs[g]], land_y.at[g * 3 + k - 1], near(1, k))
+            elif g == 0:
+                row, axis = (to_zs, to_xs)[part - 1][0], (2, 0)[part - 1]
+                for h in range(2):
+                    rows_sent[part, 0, h] = send(grads.at[part, plane, row, pl.ds(2 * h, 2)],
+                                                 land_row.at[(part - 1) * 3, pl.ds(2 * h, 2)], near(axis, (1, 3)[h]))
             elif g < 3:
-                row = (to_zs if part == 1 else to_xs)[g]
+                row = (to_zs, to_xs)[part - 1][g]
+                rows_sent[part, 0, g - 1].wait_recv()
+                spot = pl.ds(2 * (g - 1), 2)
+                add_to(grads.at[part, plane, row, spot], land_row.at[(part - 1) * 3, spot])
                 rows_sent[part, g] = send(
                     grads.at[part, plane, row], land_row.at[(part - 1) * 3 + g], near((2, 0)[part - 1], off[g]))
 
@@ -438,10 +470,10 @@
             pieces_sent[0, g] = send(piece, land_piece.at[g], near(0, off[g]))
 
     def row_in(part):
-        for g in range(3):
+        for g in (1, 2):
             rows_sent[part, g].wait_recv()
         plane, row = (x, z) if part == 1 else (y, x)
-        add_to(grads.at[part, plane, row], *[land_row.at[(part - 1) * 3 + g] for g in range(3)])
+        add_to(grads.at[part, plane, row], *[land_row.at[(part - 1) * 3 + g] for g in (1, 2)])
         axis = (1, 2)[part - 1]
         for g in range(3):
             pieces_sent[part, g] = send(grads.at[part, plane, row, wrap(at[axis] + off[g], RING)],
@@ -465,32 +497,15 @@
             for q in range(4):
                 begin_each((1,), q, 0)
 
-    for copy in w_x:
-        copy.wait_recv()
-    wx[0] = wx[0] + wx[1] + wx[2] + wx[3]
-    wcore_out[0:32, :] = wx[0, pl.ds(pl.multiple_of((1 - core) * 32, 32), 32), :]
-    wcore_out[32:40, :] = wx[0, 64:72, :]
-    w_core = send(wcore_out, wcore, partner)
-
-    begin_each(range(3), 0, 1)
-    pass_on(0)
-    w_core.wait_recv()
-    wcore[0:32, :] = wcore[0:32, :] + wx[0, pl.ds(pl.multiple_of(core * 32, 32), 32), :]
-    wcore[32:40, :] = wcore[32:40, :] + wx[0, 64:72, :]
-    whi_out[0:16, :] = wcore[pl.ds(pl.multiple_of((1 - y_hi) * 16, 16), 16), :]
-    whi_out[16:24, :] = wcore[32:40, :]
-    w_hi = send(whi_out, whi, across)
-
-    begin_each(range(3), 1, 1)
-    pass_on(1)
     w_hi.wait_recv()
     wrep[rep, 0:16, :] = whi[0:16, :] + wcore[pl.ds(pl.multiple_of(y_hi * 16, 16), 16), :]
     wrep[rep, 16:24, :] = whi[16:24, :] + wcore[32:40, :]
     w_rep = [send(wrep.at[rep], wrep.at[rep], peer(k)) for k in range(1, REPS)]
 
-    begin_each(range(3), 2, 1)
-    pass_on(2)
-    settle(0)
+    begin_each(range(3), 0, 1)
+    pass_on(0)
+    begin_each(range(3), 1, 1)
+    pass_on(1)
     for copy in w_rep:
         copy.wait_recv()
     wfull = wrep[0]
@@ -507,17 +522,22 @@
     ref = wrows(x * 64 + core * 32 + y_hi * 16, 16)
     w_hi = send(ref, ref, across)
 
+    begin_each(range(3), 2, 1)
+    pass_on(2)
+    settle(0)
+    w_hi.wait_recv()
+    ref = wrows(x * 64 + core * 32, 32)
+    w_core = send(ref, ref, partner)
+
     begin_each(range(3), 3, 1)
     pass_on(3)
     settle(1)
-    w_hi.wait_recv()
-    ref = wrows(x * 64 + core * 32, 32)
-    w_core = send(ref, ref, partner)
-    column_in(0)
-    settle(2)
     w_core.wait_recv()
     ref = wrows(x * 64, 64)
     w_x = [send(ref, ref, near(0, k)) for k in range(1, RING)]
+
+    column_in(0)
+    settle(2)
     column_in(1)
     settle(3)
     row_in(1)
@@ -601,7 +621,7 @@
             pltpu.VMEM((REPS, 24, HID), F32),
             pltpu.VMEM((HID, HID), F32),
             pltpu.VMEM((1, HID), F32),
-            pltpu.SemaphoreType.DMA((512,)),
+            pltpu.SemaphoreType.DMA((640,)),
         ],
         compiler_params=pltpu.CompilerParams(
             collective_id=0, has_side_effects=True, vmem_limit_bytes=61 * 1024 * 1024),

time: 105 us -> 99.8 us (0.950)
  Pallas kernels: 104 us -> 99 us
    pallas_call x1, Pallas kernels: 102 us -> 97.2 us  [body(): call(features, weight, bias.reshape(1, HID), adj_tiles.reshape(BLOCKS * S...]
where the time goes in v4:
time: 99.8 us; the launch traced here: 99.6 us
  Pallas kernels  99 us (99%)
    pallas_call x1, Pallas kernels, body(): call(features, weight, bias.reshape(1, HID), adj_tiles.reshape(BLOCKS * S...  97.2 us

profile of v4, /device:TPU:0, one launch (start us, length us, event | category | flops | bytes accessed | tf_op | source)
XLA Modules:
  0.0 99.6 jit_solution(9552726283297719606)
XLA Ops:
  0.6 97.2 %shard_map.102 = (bf16[192,256]{1,0:T(8,128)(2,1)}, bf16[192,256]{1,0:T(8,128)(2,1)}, f32[256,256]{1,0:T(8,128)}, f32[1,256]{1,0:T(1,128)}) custom-call(bf16[192,256]{1,0:T(8,128)(2,1)} %refs_0_.1, bf16[256,256]{1,0:T(8,128)(2,1)} %refs_1_.1, f32[1,256]{1,0:T(1,128)} %bitcast.6, bf16[96,2,128,128]{3,2,1,0:T(8,128)(2,1)} %bitcast.4, s32[12,1,16]{2,1,0:T(1,128)} %bitcast.5, ...), custom_call_target="tpu_custom_call" | custom-call | tf_op jit(solution)/shard_map/pallas_call | solution.py:629
  97.8 1.8 %shard_map.103 = (bf16[192,256]{1,0:T(8,128)(2,1)}, bf16[192,256]{1,0:T(8,128)(2,1)}, f32[256,256]{1,0:T(8,128)}, f32[1,256]{1,0:T(1,128)}) custom-call(bf16[192,256]{1,0:T(8,128)(2,1)} %get-tuple-element.12.refs_0_, bf16[192,256]{1,0:T(8,128)(2,1)} %get-tuple-element.13.refs_1_, f32[256,256]{1,0:T(8,128)} %get-tuple-element.14.refs_2_, ...), custom_call_target="tpu_custom_call" | custom-call | tf_op jit(solution)/shard_map/pallas_call | solution.py:632

commit v5 on v4

--- a/solution.py
+++ b/solution.py
@@ -279,16 +279,23 @@
 
     swap, slots = [], []
     order = (2, 1, 3, 0)
+    base = [wrap(z + dz, RING) for dz in order]
+
+    def theirs_out(g):
+        lax.fori_loop(base[g] * 3, base[g] * 3 + 3, their_block, 0)
+        rows = pl.ds(pl.multiple_of(base[g] * 384, 384), 384)
+        swap.append(send(theirs.at[rows], arrived.at[rows], partner))
+
+    theirs_out(0)
+    theirs_out(1)
     for g in range(4):
-        base = wrap(z + order[g], RING)
-        lax.fori_loop(base * 3, base * 3 + 3, their_block, 0)
-        rows = pl.ds(pl.multiple_of(base * 384, 384), 384)
-        swap.append(send(theirs.at[rows], arrived.at[rows], partner))
-        if g:
-            swap[g - 1].wait_recv()
+        lax.fori_loop(base[g] * 3, base[g] * 3 + 3, my_block, 0)
+        if g < 2:
+            theirs_out(g + 2)
+        if g < 3:
+            swap[g].wait_recv()
             for dy in (1, 0):
-                slots.append((order[g - 1], dy, share(order[g - 1], dy)))
-        lax.fori_loop(base * 3, base * 3 + 3, my_block, 0)
+                slots.append((order[g], dy, share(order[g], dy)))
     swap[3].wait_recv()
     earlier = started[:-5]
     del started[:-5]

time: 99.8 us -> 99.7 us (level)
  no operation moved by 1% of the time
where the time goes in v5:
time: 99.7 us; the launch traced here: 99.6 us
  Pallas kernels  99 us (99%)
    pallas_call x1, Pallas kernels, body(): call(features, weight, bias.reshape(1, HID), adj_tiles.reshape(BLOCKS * S...  97.1 us

profile of v5, /device:TPU:0, one launch (start us, length us, event | category | flops | bytes accessed | tf_op | source)
XLA Modules:
  0.0 99.6 jit_solution(15235665507359067379)
XLA Ops:
  0.6 97.1 %shard_map.102 = (bf16[192,256]{1,0:T(8,128)(2,1)}, bf16[192,256]{1,0:T(8,128)(2,1)}, f32[256,256]{1,0:T(8,128)}, f32[1,256]{1,0:T(1,128)}) custom-call(bf16[192,256]{1,0:T(8,128)(2,1)} %refs_0_.1, bf16[256,256]{1,0:T(8,128)(2,1)} %refs_1_.1, f32[1,256]{1,0:T(1,128)} %bitcast.6, bf16[96,2,128,128]{3,2,1,0:T(8,128)(2,1)} %bitcast.4, s32[12,1,16]{2,1,0:T(1,128)} %bitcast.5, ...), custom_call_target="tpu_custom_call" | custom-call | tf_op jit(solution)/shard_map/pallas_call | solution.py:636
  97.8 1.8 %shard_map.103 = (bf16[192,256]{1,0:T(8,128)(2,1)}, bf16[192,256]{1,0:T(8,128)(2,1)}, f32[256,256]{1,0:T(8,128)}, f32[1,256]{1,0:T(1,128)}) custom-call(bf16[192,256]{1,0:T(8,128)(2,1)} %get-tuple-element.12.refs_0_, bf16[192,256]{1,0:T(8,128)(2,1)} %get-tuple-element.13.refs_1_, f32[256,256]{1,0:T(8,128)} %get-tuple-element.14.refs_2_, ...), custom_call_target="tpu_custom_call" | custom-call | tf_op jit(solution)/shard_map/pallas_call | solution.py:639
